TPU v7x, 32 devices: a whole 2x2x4 slice. The times are simulated.
32 devices in a mesh: wide: 8 (over z, x), narrow: 4 (over y, core).
Axes of the slice: x: 2, y: 2, z: 4, core: 2. Of those that a mesh axis runs over, the one named last changes fastest.
Arguments:
- inputs: bfloat16 [12288, 768], P(('wide', 'narrow')), may hold values from -6 to 6
- lengths: int32 [32], P(('wide', 'narrow')), may hold values from 1 to 384, 9216 in all
- triple_weight: bfloat16 [768, 2304], P(('wide', 'narrow')), may hold values from -0.21875 to 0.21875
- triple_bias: bfloat16 [2304], P(('wide', 'narrow')), may hold values from -1.796875 to 1.796875
- mix_weight: bfloat16 [768, 768], P(('wide', 'narrow')), may hold values from -1.75 to 1.75
- mix_bias: bfloat16 [768], P(('wide', 'narrow')), may hold values from -1.796875 to 1.796875
- first_gain: bfloat16 [768], P(('wide', 'narrow')), may hold values from 0.25 to 1.75
- first_shift: bfloat16 [768], P(('wide', 'narrow')), may hold values from -1.796875 to 1.796875
- up_weight: bfloat16 [768, 3072], P('wide', 'narrow'), may hold values from -0.21875 to 0.21875
- up_bias: bfloat16 [3072], P('narrow'), may hold values from -1.796875 to 1.796875
- down_weight: bfloat16 [3072, 768], P('narrow', 'wide'), may hold values from -0.109375 to 0.109375
- down_bias: bfloat16 [768], P('wide'), may hold values from -1.796875 to 1.796875
- second_gain: bfloat16 [768], P(('wide', 'narrow')), may hold values from 0.25 to 1.75
- second_shift: bfloat16 [768], P(('wide', 'narrow')), may hold values from -1.796875 to 1.796875
- cotangent: bfloat16 [12288, 768], P(('wide', 'narrow')), may hold values from -6 to 6
Outputs:
- outputs: bfloat16 [12288, 768], P(('wide', 'narrow'))
- input_grad: bfloat16 [12288, 768], P(('wide', 'narrow'))
- triple_weight_grad: float32 [768, 2304], P(('wide', 'narrow'))
- triple_bias_grad: float32 [2304], P(('wide', 'narrow'))
- mix_weight_grad: float32 [768, 768], P(('wide', 'narrow'))
- mix_bias_grad: float32 [768], P(('wide', 'narrow'))
- first_gain_grad: float32 [768], P(('wide', 'narrow'))
- first_shift_grad: float32 [768], P(('wide', 'narrow'))
- up_weight_grad: float32 [768, 3072], P('wide', 'narrow')
- up_bias_grad: float32 [3072], P('narrow')
- down_weight_grad: float32 [3072, 768], P('narrow', 'wide')
- down_bias_grad: float32 [768], P('wide')
- second_gain_grad: float32 [768], P(('wide', 'narrow'))
- second_shift_grad: float32 [768], P(('wide', 'narrow'))
Inputs may be any that keep to these rules, and one draw needn't show every extreme that they name: `lengths`: entry b is the number of live tokens of the sequence in row block b; the rest of the block is padding. Some sequence fills its block.
All inputs are finite; a program needn't handle non-finite values.
Results may differ from a plain program's by a relative error of at most 0.017.
Values may be sent and summed in bfloat16 or wider, within the bound.
No kernel may reach another device: no remote copies, remote signals or barrier semaphores. Data moves between devices by JAX's collectives and lax.ppermute only.
A program may use at most 128 MiB of HBM per device.

v0:
```python
import math

import jax
import jax.numpy as jnp
from jax import lax
from jax.sharding import PartitionSpec as P

H = 12
HD = 64


EPSILON = 1e-06


def tables(token_rows, width, head):
    position = jnp.arange(token_rows, dtype=jnp.float32)
    column = jnp.arange(width, dtype=jnp.int32)
    pair_index = (column % head // 2).astype(jnp.float32)
    frequency = jnp.exp(pair_index * (-2.0 / head) * math.log(10000.0))
    angle = position[:, None] * frequency[None, :]
    parity = (column % 2).astype(jnp.float32) * 2.0 - 1.0
    return (jnp.cos(angle), jnp.sin(angle) * parity[None, :])


def swapped(values):
    shape = values.shape
    paired = values.reshape(shape[:-1] + (shape[-1] // 2, 2))
    return paired[..., ::-1].reshape(shape)


def rotate(values, cosine, sine):
    return values * cosine + swapped(values) * sine


def unrotate(grad, cosine, sine):
    return grad * cosine + swapped(grad * sine)


def normalize_forward(values, gain, shift):
    mean_row = jnp.mean(values, -1, keepdims=True)
    centred = values - mean_row
    inverse = lax.rsqrt(jnp.mean(centred * centred, -1, keepdims=True) + EPSILON)
    unit = centred * inverse
    return (unit * gain + shift, unit, inverse)


def normalize_backward(grad, unit, inverse, gain):
    scaled = grad * gain
    inner = (
        scaled
        - jnp.mean(scaled, -1, keepdims=True)
        - unit * jnp.mean(scaled * unit, -1, keepdims=True)
    )
    return (inner * inverse, jnp.sum(grad * unit, 0), jnp.sum(grad, 0))


def gelu_exact(values):
    return jax.nn.gelu(values, approximate=False)


def gelu_backward(upward, grad_active):
    unused, pull_back = jax.vjp(gelu_exact, upward)
    return pull_back(grad_active)[0]


def softmax_block(query_block, key, valid, scale):
    scores = (
        jnp.einsum("qhd,khd->hqk", query_block, key, preferred_element_type=jnp.float32) * scale
    )
    scores = jnp.where(valid[None, None, :], scores, -1e30)
    return jax.nn.softmax(scores, axis=-1)


def attention_forward(query, key, value, valid, scale):
    token_rows = query.shape[0]
    block = min(512, token_rows)
    weights_block = softmax_block(query, key, valid, scale)
    context = jnp.einsum(
        "hqk,khd->qhd",
        weights_block.astype(jnp.bfloat16),
        value,
        preferred_element_type=jnp.float32,
    )
    pieces = context.reshape(block, -1).astype(jnp.bfloat16)
    return pieces


def attention_backward(query, key, value, grad_context, valid, scale):
    weights_block = softmax_block(query, key, valid, scale)
    grad_weights = jnp.einsum(
        "qhd,khd->hqk", grad_context, value, preferred_element_type=jnp.float32
    )
    inner = weights_block * (
        grad_weights - jnp.sum(weights_block * grad_weights, -1, keepdims=True)
    )
    inner_low = inner.astype(jnp.bfloat16)
    query_pieces = (
        jnp.einsum("hqk,khd->qhd", inner_low, key, preferred_element_type=jnp.float32) * scale
    )
    grad_key = (
        jnp.einsum("hqk,qhd->khd", inner_low, query, preferred_element_type=jnp.float32) * scale
    )
    grad_value = jnp.einsum(
        "hqk,qhd->khd",
        weights_block.astype(jnp.bfloat16),
        grad_context,
        preferred_element_type=jnp.float32,
    )
    return (query_pieces, grad_key, grad_value)


def body(
    inputs,
    lengths,
    triple_weight,
    triple_bias,
    mix_weight,
    mix_bias,
    first_gain,
    first_shift,
    up_weight,
    up_bias,
    down_weight,
    down_bias,
    second_gain,
    second_shift,
    cotangent,
):
    token_rows, width = inputs.shape
    scale = 1.0 / math.sqrt(HD)
    head_shape = (token_rows, H, HD)
    (
        triple_full,
        mix_full,
        triple_bias_full,
        mix_bias_full,
        gain_one,
        shift_one,
        gain_two,
        shift_two,
    ) = (
        lax.all_gather(triple_weight, ("wide", "narrow"), axis=0, tiled=True),
        lax.all_gather(mix_weight, ("wide", "narrow"), axis=0, tiled=True),
        lax.all_gather(triple_bias, ("wide", "narrow"), axis=0, tiled=True),
        lax.all_gather(mix_bias, ("wide", "narrow"), axis=0, tiled=True),
        lax.all_gather(first_gain, ("wide", "narrow"), axis=0, tiled=True),
        lax.all_gather(first_shift, ("wide", "narrow"), axis=0, tiled=True),
        lax.all_gather(second_gain, ("wide", "narrow"), axis=0, tiled=True),
        lax.all_gather(second_shift, ("wide", "narrow"), axis=0, tiled=True),
    )
    up_rows, down_columns, down_bias_full = (
        lax.all_gather(up_weight, "wide", axis=0, tiled=True),
        lax.all_gather(down_weight, "wide", axis=1, tiled=True),
        lax.all_gather(down_bias, "wide", axis=0, tiled=True),
    )
    gain_one = gain_one.astype(jnp.float32)
    gain_two = gain_two.astype(jnp.float32)
    cosine, sine = tables(token_rows, width, HD)
    valid = jnp.arange(token_rows, dtype=jnp.int32) < lengths[0]
    triple = jnp.dot(
        inputs, triple_full, preferred_element_type=jnp.float32
    ) + triple_bias_full.astype(jnp.float32)
    query = rotate(triple[:, :width], cosine, sine).astype(jnp.bfloat16).reshape(head_shape)
    key = (
        rotate(triple[:, width : 2 * width], cosine, sine).astype(jnp.bfloat16).reshape(head_shape)
    )
    value = triple[:, 2 * width :].astype(jnp.bfloat16).reshape(head_shape)
    context = attention_forward(query, key, value, valid, scale)
    branch = jnp.dot(context, mix_full, preferred_element_type=jnp.float32) + mix_bias_full.astype(
        jnp.float32
    )
    first, first_unit, first_inverse = normalize_forward(
        inputs.astype(jnp.float32) + branch, gain_one, shift_one.astype(jnp.float32)
    )
    first_low = first.astype(jnp.bfloat16)
    gathered = lax.all_gather(first_low, "narrow", axis=0, tiled=True)
    upward = jnp.dot(gathered, up_rows, preferred_element_type=jnp.float32) + up_bias.astype(
        jnp.float32
    )
    active = gelu_exact(upward).astype(jnp.bfloat16)
    downward = lax.psum_scatter(
        jnp.dot(active, down_columns, preferred_element_type=jnp.float32).astype(jnp.bfloat16),
        "narrow",
        scatter_dimension=0,
        tiled=True,
    ).astype(jnp.float32)
    downward = downward + down_bias_full.astype(jnp.float32)
    result, second_unit, second_inverse = normalize_forward(
        first + downward, gain_two, shift_two.astype(jnp.float32)
    )
    outputs = result.astype(jnp.bfloat16)
    grad_second, second_gain_grad, second_shift_grad = normalize_backward(
        cotangent.astype(jnp.float32), second_unit, second_inverse, gain_two
    )
    grad_down = grad_second.astype(jnp.bfloat16)
    grad_gathered = lax.all_gather(grad_down, "narrow", axis=0, tiled=True)
    grad_active = jnp.dot(grad_gathered, down_columns.T, preferred_element_type=jnp.float32)
    grad_up = gelu_backward(upward, grad_active).astype(jnp.bfloat16)
    grad_feed = lax.psum_scatter(
        jnp.dot(grad_up, up_rows.T, preferred_element_type=jnp.float32).astype(jnp.bfloat16),
        "narrow",
        scatter_dimension=0,
        tiled=True,
    ).astype(jnp.float32)
    up_part = jnp.dot(gathered.T, grad_up, preferred_element_type=jnp.float32)
    down_part = jnp.dot(active.T, grad_gathered, preferred_element_type=jnp.float32)
    down_bias_part = jnp.sum(grad_gathered, 0, dtype=jnp.float32)
    up_weight_grad, down_weight_grad, down_bias_grad = (
        lax.psum_scatter(
            up_part.astype(jnp.bfloat16), "wide", scatter_dimension=0, tiled=True
        ).astype(jnp.float32),
        lax.psum_scatter(
            down_part.astype(jnp.bfloat16), "wide", scatter_dimension=1, tiled=True
        ).astype(jnp.float32),
        lax.psum_scatter(
            down_bias_part.astype(jnp.bfloat16), "wide", scatter_dimension=0, tiled=True
        ).astype(jnp.float32),
    )
    up_bias_grad = lax.psum(jnp.sum(grad_up, 0, dtype=jnp.float32), "wide")
    grad_first = grad_second + grad_feed
    grad_middle, first_gain_grad, first_shift_grad = normalize_backward(
        grad_first, first_unit, first_inverse, gain_one
    )
    grad_branch = grad_middle.astype(jnp.bfloat16)
    mix_weight_grad = jnp.dot(context.T, grad_branch, preferred_element_type=jnp.float32)
    mix_bias_grad = jnp.sum(grad_branch, 0, dtype=jnp.float32)
    triple_back, mix_back = (
        lax.all_gather(triple_weight, ("wide", "narrow"), axis=0, tiled=True),
        lax.all_gather(mix_weight, ("wide", "narrow"), axis=0, tiled=True),
    )
    grad_context = (
        jnp.dot(grad_branch, mix_back.T, preferred_element_type=jnp.float32)
        .astype(jnp.bfloat16)
        .reshape(head_shape)
    )
    grad_query, grad_key, grad_value = attention_backward(
        query, key, value, grad_context, valid, scale
    )
    grad_triple = jnp.concatenate(
        [
            unrotate(grad_query.reshape(token_rows, width), cosine, sine),
            unrotate(grad_key.reshape(token_rows, width), cosine, sine),
            grad_value.reshape(token_rows, width),
        ],
        1,
    ).astype(jnp.bfloat16)
    triple_local = jnp.dot(inputs.T, grad_triple, preferred_element_type=jnp.float32)
    triple_bias_local = jnp.sum(grad_triple, 0, dtype=jnp.float32)
    grad_inputs = grad_middle + jnp.dot(
        grad_triple, triple_back.T, preferred_element_type=jnp.float32
    )
    summed = (
        lax.psum_scatter(triple_local, ("wide", "narrow"), scatter_dimension=0, tiled=True),
        lax.psum_scatter(mix_weight_grad, ("wide", "narrow"), scatter_dimension=0, tiled=True),
        lax.psum_scatter(triple_bias_local, ("wide", "narrow"), scatter_dimension=0, tiled=True),
        lax.psum_scatter(mix_bias_grad, ("wide", "narrow"), scatter_dimension=0, tiled=True),
        lax.psum_scatter(first_gain_grad, ("wide", "narrow"), scatter_dimension=0, tiled=True),
        lax.psum_scatter(first_shift_grad, ("wide", "narrow"), scatter_dimension=0, tiled=True),
        lax.psum_scatter(second_gain_grad, ("wide", "narrow"), scatter_dimension=0, tiled=True),
        lax.psum_scatter(second_shift_grad, ("wide", "narrow"), scatter_dimension=0, tiled=True),
    )
    return (
        outputs,
        grad_inputs.astype(jnp.bfloat16),
        summed[0],
        summed[2],
        summed[1],
        summed[3],
        summed[4],
        summed[5],
        up_weight_grad,
        up_bias_grad,
        down_weight_grad,
        down_bias_grad,
        summed[6],
        summed[7],
    )


def solution(mesh):
    placed = (
        P(("wide", "narrow"), None),
        P(("wide", "narrow")),
        P(("wide", "narrow"), None),
        P(("wide", "narrow")),
        P(("wide", "narrow"), None),
        P(("wide", "narrow")),
        P(("wide", "narrow")),
        P(("wide", "narrow")),
        P("wide", "narrow"),
        P("narrow"),
        P("narrow", "wide"),
        P("wide"),
        P(("wide", "narrow")),
        P(("wide", "narrow")),
        P(("wide", "narrow"), None),
    )
    return jax.shard_map(
        body,
        mesh=mesh,
        in_specs=placed,
        out_specs=(
            P(("wide", "narrow"), None),
            P(("wide", "narrow"), None),
            P(("wide", "narrow"), None),
            P(("wide", "narrow")),
            P(("wide", "narrow"), None),
            P(("wide", "narrow")),
            P(("wide", "narrow")),
            P(("wide", "narrow")),
            P("wide", "narrow"),
            P("narrow"),
            P("narrow", "wide"),
            P("wide"),
            P(("wide", "narrow")),
            P(("wide", "narrow")),
        ),
        check_vma=False,
    )
```

profile of v0, /device:TPU:0, one launch (start us, length us, event | category | flops | bytes accessed | tf_op | source)
XLA Modules:
  0.0 723.4 jit_solution(7798430704775976542)
XLA Ops:
  14.5 42.5 %all-reduce.15 = (bf16[2304]{0:T(1024)(128)(2,1)S(1)}, bf16[768]{0:T(1024)(128)(2,1)S(1)}, bf16[768]{0:T(1024)(128)(2,1)S(1)}, bf16[768]{0:T(1024)(128)(2,1)S(1)...) all-reduce(bf16[2304]{0:T(1024)(128)(2,1)S(1)} %dynamic-update-slic, ...), channel_id=1, replica_groups=mesh['wide'=8,'narrow'=4] {'wide','narrow'}, use_global_device_ids=true, to_apply=%add | all-reduce | flops 6144 | bytes 24576
  59.4 14.5 %all-gather.7.cloned.1.call-done = bf16[768,2304]{1,0:T(8,128)(2,1)} async-done(((bf16[24,2304]{1,0:T(8,128)(2,1)}), bf16[768,2304]{1,0:T(8,128)(2,1)}) %all-gather.7.cloned.1.call-update) | async-done | bytes 3538960 | tf_op jit(solution)/shard_map/all_gather | solution.py:142
  87.8 6.6 rev.13
  105.6 6.6 rev.12
  118.1 7.8 %add_convert_fusion.4 = (bf16[384,768]{1,0:T(8,128)(2,1)}, bf16[384,768]{1,0:T(8,128)(2,1)}) fusion(f32[384,768]{1,0:T(8,128)} %copy.88, f32[768]{0:T(1024)S(1)} %get-tuple-element.119, f32[768]{0:T(1024)S(1)} %get-tuple-element.118, f32[384,2304]{1,0:T(8,128)S(1)} %convolution_add_fusion, f32[384,768]{1,0:T(8,128)} %copy.85), kind=kLoop, calls=%fused_computation.73 | loop fusion | flops 2949120 | bytes 5904384 | tf_op jit(solution)/shard_map/convert_element_type | solution.py:165
  129.0 4.6 fusion.66
  142.1 29.8 %all-gather.13.cloned.1.call-done = bf16[768,768]{1,0:T(8,128)(2,1)} async-done(((bf16[96,768]{1,0:T(8,128)(2,1)}), bf16[768,768]{1,0:T(8,128)(2,1)}) %all-gather.13.cloned.1.call-update) | async-done | bytes 1179664 | tf_op jit(solution)/shard_map/all_gather | solution.py:152
  171.9 24.9 %all-gather.11.cloned.1.call-done = bf16[1536,768]{1,0:T(8,128)(2,1)} async-done(((bf16[384,768]{1,0:T(8,128)(2,1)}), bf16[1536,768]{1,0:T(8,128)(2,1)}) %all-gather.11.cloned.1.call-update) | async-done | bytes 2359312 | tf_op jit(solution)/shard_map/all_gather | solution.py:176
  196.8 15.0 %multiply_convert_fusion.1 = (bf16[1536,768]{1,0:T(8,128)(2,1)}, f32[1536,768]{1,0:T(8,128)}, f32[1536,768]{1,0:T(8,128)}) fusion(f32[768]{0:T(1024)S(1)} %convert_element_type.166, bf16[1536,768]{1,0:T(8,128)(2,1)} %all-gather.11.cloned.1.call-done, bf16[768,768]{1,0:T(8,128)(2,1)} %all-gather.13.cloned.1.call-done), kind=kOutput, calls=%fused_computation.11 | convolution fusion | flops 1889796096 | bytes 15338496 | tf_op jit(solution)/shard_map/dot_general | solution.py:177
  211.8 28.1 %all-gather.15.cloned.1.call-done = bf16[768,768]{0,1:T(8,128)(2,1)} async-done(((bf16[768,96]{0,1:T(8,128)(2,1)}), bf16[768,768]{0,1:T(8,128)(2,1)}) %all-gather.15.cloned.1.call-update) | async-done | bytes 1179664 | tf_op jit(solution)/shard_map/all_gather | solution.py:153
  239.9 5.5 convolution_convert_fusion.1
  247.5 19.2 %all-reduce.4 = bf16[768]{0:T(1024)(128)(2,1)S(1)} all-reduce(bf16[768]{0:T(1024)(128)(2,1)S(1)} %dynamic-update-slice.4), channel_id=1, replica_groups=mesh['wide'=8,'narrow'=4] {'wide'}, use_global_device_ids=true, to_apply=%add.4 | all-reduce | flops 768 | bytes 3072
  266.8 10.6 %reduce-scatter.9.cloned.1.call-done = bf16[384,768]{1,0:T(8,128)(2,1)} async-done(((bf16[1536,768]{1,0:T(8,128)(2,1)}), bf16[384,768]{1,0:T(8,128)(2,1)}) %reduce-scatter.9.cloned.1.call-update) | async-done | bytes 589840 | tf_op jit(solution)/shard_map/reduce_scatter | solution.py:181
  282.1 24.0 %all-gather.17.cloned.1.call-done = bf16[1536,768]{1,0:T(8,128)(2,1)} async-done(((bf16[384,768]{1,0:T(8,128)(2,1)}), bf16[1536,768]{1,0:T(8,128)(2,1)}) %all-gather.17.cloned.1.call-update) | async-done | bytes 2359312 | tf_op jit(solution)/shard_map/all_gather | solution.py:196
  306.1 8.8 %convert_reduce_fusion = (f32[768]{0:T(1024)}, bf16[1536,768]{1,0:T(8,128)(2,1)S(1)}) fusion(f32[1536,768]{1,0:T(8,128)} %get-tuple-element.99, f32[1536,768]{1,0:T(8,128)} %get-tuple-element.115, f32[768]{0:T(1024)S(1)} %convert_element_type.166, bf16[1536,768]{1,0:T(8,128)(2,1)} %all-gather.17.cloned.1.call-done, ...), kind=kOutput, calls=%fused_computation.9 | convolution fusion | flops 1831992576 | bytes 15341568 | tf_op jit(solution)/shard_map/dot_general | solution.py:197
  319.9 5.5 convolution_convert_fusion.3
  327.2 5.9 convolution_convert_fusion.2
  333.3 19.8 %reduce-scatter.11.cloned.1.call-done = bf16[384,768]{1,0:T(8,128)(2,1)} async-done(((bf16[1536,768]{1,0:T(8,128)(2,1)}), bf16[384,768]{1,0:T(8,128)(2,1)}) %reduce-scatter.11.cloned.1.call-update) | async-done | bytes 589840 | tf_op jit(solution)/shard_map/reduce_scatter | solution.py:199
  360.2 7.7 %multiply_reduce_fusion = (f32[12,384]{1,0:T(8,128)}, f32[12,384,384]{1,2,0:T(8,128)}) fusion(f32[12,384,384]{1,2,0:T(8,128)} %get-tuple-element.112, f32[12,384]{1,0:T(8,128)S(1)} %copy-done.24, bf16[384,12,64]{0,2,1:T(8,128)(2,1)S(1)} %bitcast.81, bf16[384,12,64]{0,2,1:T(8,128)(2,1)S(1)} %bitcast.80), kind=kOutput, calls=%fused_computation.2 | convolution fusion | flops 231796224 | bytes 15372288 | tf_op jit(solution)/shard_map/qhd,khd->hqk/dot_general | solution.py:90
  368.0 4.4 fusion.23
  373.5 6.2 multiply_convert_fusion
  390.1 18.8 %fusion.33 = (f32[384,384,2]{0,2,1:T(2,128)S(1)}, f32[384,384,2]{0,2,1:T(2,128)}) fusion(f32[384,384,2]{0,2,1:T(2,128)S(1)} %copy-done.4, f32[384,2]{1,0:T(8,128)} %copy.95, f32[384,2]{1,0:T(8,128)} %copy.94, f32[384,384,2]{0,2,1:T(2,128)S(1)} %reshape.212), kind=kLoop, calls=%fused_computation.83 | loop fusion | flops 1179648 | bytes 4724736 | tf_op jit(solution)/shard_map/mul | solution.py:36
  415.9 6.7 rev.15
  429.8 5.4 add_convert_fusion.2
  436.3 5.0 convolution_bitcast_fusion
  441.3 8.1 %copy.107 = f32[768,2304]{1,0:T(8,128)} copy(f32[768,2304]{0,1:T(8,128)} %convolution_bitcast_fusion) | data formatting | bytes 14155776
  452.4 21.3 %all-reduce.11 = bf16[768]{0:T(1024)(128)(2,1)S(1)} all-reduce(bf16[768]{0:T(1024)(128)(2,1)S(1)} %reduce_sum.184), channel_id=12, replica_groups=mesh['wide'=8,'narrow'=4] {'wide'}, use_global_device_ids=true, to_apply=%region_28.29.clone | all-reduce | flops 768 | bytes 3072
  473.7 17.7 %psum.7 = f32[768]{0:T(1024)} all-reduce(f32[768]{0:T(1024)S(1)} %copy-done.30), channel_id=1, replica_groups=mesh['wide'=8,'narrow'=4] {'wide'}, use_global_device_ids=true, to_apply=%region_25.26 | all-reduce | flops 768 | bytes 6144 | tf_op jit(solution)/shard_map/psum | solution.py:219
  495.7 38.0 %all-reduce.14 = (f32[2304]{0:T(1024)S(1)}, f32[768]{0:T(1024)S(1)}, f32[768]{0:T(1024)S(1)}, f32[768]{0:T(1024)S(1)}, f32[768]{0:T(1024)S(1)}, /*index=5*/f32[768]{0:T(1024)S(1)}) all-reduce(f32[2304]{0:T(1024)S(1)} %convert_reduce_fusion.1, f32[768]{0:T(1024)S(1)} %copy-done.28, ...), channel_id=5, replica_groups=mesh['wide'=8,'narrow'=4] {'wide','narrow'}, use_global_device_ids=true, to_apply=%region_15.16.clone | all-reduce | flops 6144 | bytes 49152
  537.2 4.4 fusion.19
  541.5 49.3 %reduce-scatter.13.cloned.1.call-done = f32[24,768]{1,0:T(8,128)} async-done(((f32[768,768]{1,0:T(8,128)}), f32[24,768]{1,0:T(8,128)}) %reduce-scatter.13.cloned.1.call-update) | async-done | bytes 73744 | tf_op jit(solution)/shard_map/reduce_scatter | solution.py:254
  590.8 125.3 %reduce-scatter.19.cloned.1.call-done = f32[24,2304]{1,0:T(8,128)} async-done(((f32[768,2304]{1,0:T(8,128)}), f32[24,2304]{1,0:T(8,128)}) %reduce-scatter.19.cloned.1.call-update) | async-done | bytes 221200
  (197 shorter events, 108.3 us)
Async XLA Ops:
  7.2 66.7 %all-gather.7.cloned.1.call-start = ((), (), s32[]{:S(2)}) async-start(), calls=%async_computation.6 | async-start | bytes 3649536 | tf_op jit(solution)/shard_map/all_gather | solution.py:142
  7.9 129.5 %all-gather.9.cloned.1.call-start = ((), (), s32[]{:S(2)}) async-start(), calls=%async_computation.7 | async-start | bytes 1216512 | tf_op jit(solution)/shard_map/all_gather | solution.py:143
  8.7 163.2 %all-gather.13.cloned.1.call-start = ((), (), s32[]{:S(2)}) async-start(), calls=%async_computation.9 | async-start | bytes 1327104 | tf_op jit(solution)/shard_map/all_gather | solution.py:152
  9.4 187.4 %all-gather.11.cloned.1.call-start = ((), (), s32[]{:S(2)}) async-start(), calls=%async_computation.8 | async-start | bytes 2949120 | tf_op jit(solution)/shard_map/all_gather | solution.py:176
  9.5 108.6 %copy-start.21 = (f32[768]{0:T(1024)}, f32[768]{0:T(1024)S(1)}, u32[]{:S(2)}) copy-start(f32[768]{0:T(1024)S(1)} %get-tuple-element.118) | copy-start | bytes 9220
  127.3 6.2 copy-start.12
  128.9 4.6 copy-start.13
  141.0 98.9 %all-gather.15.cloned.1.call-start = ((), (), s32[]{:S(2)}) async-start(), calls=%async_computation.10 | async-start | bytes 1327104 | tf_op jit(solution)/shard_map/all_gather | solution.py:153
  141.6 135.8 %reduce-scatter.9.cloned.1.call-start = ((), (), s32[]{:S(2)}) async-start(), calls=%async_computation.11 | async-start | bytes 2949120 | tf_op jit(solution)/shard_map/reduce_scatter | solution.py:181
  245.4 21.4 %copy-start.33 = (bf16[768]{0:T(1024)(128)(2,1)S(1)}, bf16[768]{0:T(1024)(128)(2,1)}, u32[]{:S(2)}) copy-start(bf16[768]{0:T(1024)(128)(2,1)} %get-tuple-element.89) | copy-start | bytes 4612
  245.4 21.4 %copy-start.32 = (bf16[768]{0:T(1024)(128)(2,1)S(1)}, bf16[768]{0:T(1024)(128)(2,1)}, u32[]{:S(2)}) copy-start(bf16[768]{0:T(1024)(128)(2,1)} %get-tuple-element.88) | copy-start | bytes 4612
  245.4 33.8 %copy-start.11 = (bf16[384,768]{1,0:T(8,128)(2,1)S(1)}, bf16[384,768]{1,0:T(8,128)(2,1)}, u32[]{:S(2)}) copy-start(bf16[384,768]{1,0:T(8,128)(2,1)} %param.29) | copy-start | bytes 1769476
  245.4 60.7 %all-gather.17.cloned.1.call-start = ((), (), s32[]{:S(2)}) async-start(), calls=%async_computation.12 | async-start | bytes 2949120 | tf_op jit(solution)/shard_map/all_gather | solution.py:196
  281.9 71.2 %reduce-scatter.11.cloned.1.call-start = ((), (), s32[]{:S(2)}) async-start(), calls=%async_computation.13 | async-start | bytes 2949120 | tf_op jit(solution)/shard_map/reduce_scatter | solution.py:199
  306.1 10.2 %copy-start.35 = (bf16[768,768]{1,0:T(8,128)(2,1)S(1)}, bf16[768,768]{1,0:T(8,128)(2,1)}, u32[]{:S(2)}) copy-start(bf16[768,768]{1,0:T(8,128)(2,1)} %all-gather.13.cloned.1.call-done) | copy-start | bytes 3538948
  319.9 172.2 %reduce-scatter.15.cloned.1.call-start = ((), (), s32[]{:S(2)}) async-start(), calls=%async_computation.15 | async-start | bytes 1327104 | tf_op jit(solution)/shard_map/reduce_scatter | solution.py:209
  325.4 168.3 %reduce-scatter.17.cloned.1.call-start = ((), (), s32[]{:S(2)}) async-start(), calls=%async_computation.16 | async-start | bytes 1327104 | tf_op jit(solution)/shard_map/reduce_scatter | solution.py:212
  333.1 257.8 %reduce-scatter.13.cloned.1.call-start = ((), (), s32[]{:S(2)}) async-start(), calls=%async_computation.14 | async-start | bytes 2433024 | tf_op jit(solution)/shard_map/reduce_scatter | solution.py:254
  367.9 348.3 %reduce-scatter.19.cloned.1.call-start = ((), (), s32[]{:S(2)}) async-start(), calls=%async_computation.17 | async-start | bytes 7299072
  373.5 6.2 copy-start.14
  422.6 5.7 copy-start
  429.8 6.5 copy-start.9
  429.8 6.5 copy-start.37
  449.4 24.4 %copy-start.30 = (f32[768]{0:T(1024)S(1)}, f32[768]{0:T(1024)}, u32[]{:S(2)}) copy-start(f32[768]{0:T(1024)} %get-tuple-element.90) | copy-start | bytes 9220
  449.4 45.9 %copy-start.6 = (bf16[384,768]{1,0:T(8,128)(2,1)S(1)}, bf16[384,768]{1,0:T(8,128)(2,1)}, u32[]{:S(2)}) copy-start(bf16[384,768]{1,0:T(8,128)(2,1)} %copy-done.5) | copy-start | bytes 1769476
  449.4 45.9 %copy-start.8 = (bf16[384,768]{1,0:T(8,128)(2,1)S(1)}, bf16[384,768]{1,0:T(8,128)(2,1)}, u32[]{:S(2)}) copy-start(bf16[384,768]{1,0:T(8,128)(2,1)} %copy-done.7) | copy-start | bytes 1769476
  449.4 45.9 %copy-start.10 = (bf16[384,768]{1,0:T(8,128)(2,1)S(1)}, bf16[384,768]{1,0:T(8,128)(2,1)}, u32[]{:S(2)}) copy-start(bf16[384,768]{1,0:T(8,128)(2,1)} %copy.101) | copy-start | bytes 1769476
  450.2 45.4 %copy-start.25 = (f32[768]{0:T(1024)S(1)}, f32[768]{0:T(1024)}, u32[]{:S(2)}) copy-start(f32[768]{0:T(1024)} %get-tuple-element.77) | copy-start | bytes 9220
  450.2 45.4 %copy-start.26 = (f32[768]{0:T(1024)S(1)}, f32[768]{0:T(1024)}, u32[]{:S(2)}) copy-start(f32[768]{0:T(1024)} %get-tuple-element.70) | copy-start | bytes 9220
  450.2 45.4 %copy-start.27 = (f32[768]{0:T(1024)S(1)}, f32[768]{0:T(1024)}, u32[]{:S(2)}) copy-start(f32[768]{0:T(1024)} %get-tuple-element.75) | copy-start | bytes 9220
  450.2 45.4 %copy-start.28 = (f32[768]{0:T(1024)S(1)}, f32[768]{0:T(1024)}, u32[]{:S(2)}) copy-start(f32[768]{0:T(1024)} %get-tuple-element.92) | copy-start | bytes 9220
  450.2 86.9 %copy-start.3 = (f32[384,768]{1,0:T(8,128)S(1)}, f32[384,768]{1,0:T(8,128)}, u32[]{:S(2)}) copy-start(f32[384,768]{1,0:T(8,128)} %copy-done.2) | copy-start | bytes 3538948
  (21 other events, 52.8 us)
Sparse Core Ops, SparseCore 0:
  10.9 62.8 all-gather.6
  76.8 52.8 all-gather.8
  131.9 39.9 all-gather.12
  173.9 22.8 all-gather.10
  198.8 41.0 all-gather.14
  245.5 31.8 reduce-scatter.8
  282.0 24.0 all-gather.16
  320.0 33.0 reduce-scatter.10
  356.5 64.0 reduce-scatter.14
  423.8 63.1 reduce-scatter.16
  492.8 97.9 reduce-scatter.12
  597.9 118.2 reduce-scatter.18
where the time goes:
time: 735 us; the launch traced here: 723 us
  waiting for transfers between devices  329 us (45%)
  blocking collectives  139 us (19%)
  local copies, waits for them, and re-layouts  93.7 us (13%)
  matrix products  87.9 us (12%)
  other arithmetic  55.5 us (8%)
  between operations  17.3 us (2%)
    unnamed x13, waiting for transfers between devices  128 us
    unnamed x4, blocking collectives  121 us
    reduce_scatter x1, waiting for transfers between devices, body(): lax.psum_scatter(mix_weight_grad, ('wide', 'narrow'), scatter_dimension=0...  49.3 us
    all_gather x1, waiting for transfers between devices, body(): lax.all_gather(up_weight, 'wide', axis=0, tiled=True)  29.8 us
    all_gather x1, waiting for transfers between devices, body(): lax.all_gather(down_weight, 'wide', axis=1, tiled=True)  28.1 us
    all_gather x1, waiting for transfers between devices, body(): gathered = lax.all_gather(first_low, 'narrow', axis=0, tiled=True)  24.9 us
    all_gather x1, waiting for transfers between devices, body(): grad_gathered = lax.all_gather(grad_down, 'narrow', axis=0, tiled=True)  24 us
    rev x4, local copies, waits for them, and re-layouts, swapped(): return paired[..., ::-1].reshape(shape)  23.1 us
  transfers between devices with their start and end apart: 12, of which 9 were waited for; matrix products, arithmetic and copies ran while one was open for 29% of the time, Pallas kernels for 0%

commit v1 on v0

--- a/solution.py
+++ b/solution.py
@@ -1,8 +1,12 @@
+import functools
 import math
 
 import jax
 import jax.numpy as jnp
+import numpy as np
 from jax import lax
+from jax.experimental import pallas as pl
+from jax.experimental.pallas import tpu as pltpu
 from jax.sharding import PartitionSpec as P
 
 H = 12
@@ -277,6 +281,979 @@
     )
 
 
+VMEM = pltpu.VMEM
+SMEM = pltpu.SMEM
+BF = jnp.bfloat16
+F32 = jnp.float32
+AXES = ("wide", "narrow")
+WHOLE = pl.BlockSpec(memory_space=VMEM)
+SCALARS = pl.BlockSpec(memory_space=SMEM)
+LEFT = pl.BlockSpec(memory_space=pltpu.HBM)
+
+
+def nn(a, b):
+    return lax.dot_general(a, b, (((1,), (0,)), ((), ())), preferred_element_type=F32)
+
+
+def nt(a, b):
+    return lax.dot_general(a, b, (((1,), (1,)), ((), ())), preferred_element_type=F32)
+
+
+def tn(a, b):
+    return lax.dot_general(a, b, (((0,), (0,)), ((), ())), preferred_element_type=F32)
+
+
+def shape(dims, dtype=BF):
+    return jax.ShapeDtypeStruct(dims, dtype)
+
+
+class Load:
+    def __init__(self, source, held, sem):
+        self.copy = pltpu.make_async_copy(source, held, sem)
+        self.held, self.waited = held, False
+        self.shape = held.shape
+        self.copy.start()
+
+    def __call__(self):
+        if not self.waited:
+            self.copy.wait()
+            self.waited = True
+        return self.held
+
+
+def call(kernel, outs, operands, kinds, scratch, flops, megabytes, out_specs=None):
+    specs = {"s": SCALARS, "v": WHOLE, "h": LEFT, "l": LEFT}
+    loads = [k for k, kind in enumerate(kinds) if kind == "l"]
+    held = [VMEM(operands[k].shape, operands[k].dtype) for k in loads]
+    assert len(kinds) == len(operands)
+
+    def whole(*refs):
+        refs = list(refs)
+        count = len(loads)
+        if count:
+            sems = refs.pop()
+            buffers, refs = refs[-count:], refs[:-count]
+            for n, k in enumerate(loads):
+                refs[k] = Load(refs[k], buffers[n], sems.at[n])
+        kernel(*refs)
+        for k in loads:
+            refs[k]()
+
+    return pl.pallas_call(
+        whole,
+        out_shape=outs,
+        in_specs=[specs[kind] for kind in kinds],
+        out_specs=[WHOLE] * len(outs) if out_specs is None else out_specs,
+        scratch_shapes=list(scratch)
+        + held
+        + ([pltpu.SemaphoreType.DMA((len(loads),))] if loads else []),
+        compiler_params=pltpu.CompilerParams(vmem_limit_bytes=megabytes << 20),
+        cost_estimate=pl.CostEstimate(
+            flops=int(flops), bytes_accessed=1, transcendentals=0
+        ),
+    )(*operands)
+
+
+def drain(ref, sem):
+    pltpu.make_async_copy(ref, ref, sem).wait()
+
+
+class Plan:
+    def __init__(self, wide, narrow):
+        self.wide, self.narrow = wide, narrow
+        self.devices = wide * narrow
+        x, y = narrow, narrow // 2
+        self.last, self.first = (y, x), (x, y)
+        self.far = wide // 2
+        self.line = self.devices // self.far
+        self.slots = 4 * self.far
+
+    def over(self, core, slot):
+        mask = self.first[core] if slot // self.far & 1 else 0
+        return mask ^ (self.last[core] if slot // self.far & 2 else 0)
+
+    def chips(self, device):
+        core = device & 1
+        return [
+            (device ^ (r % self.far * self.line) ^ self.over(c, r)) >> 1
+            for c in (core, core ^ 1)
+            for r in range(self.slots)
+        ]
+
+    def table(self, index, live):
+        chips = np.array([self.chips(i) for i in range(self.devices)], np.int32)
+        mine = lax.dynamic_slice(jnp.asarray(chips), (index, 0), (1, chips.shape[1]))[0]
+        return jnp.concatenate([mine, (index & 1)[None].astype(jnp.int32), live])
+
+    def own(self, table, slot):
+        return table[slot]
+
+    def other(self, table, slot):
+        return table[self.slots + slot]
+
+    def core(self, table):
+        return table[2 * self.slots]
+
+    def live(self, table):
+        return table[2 * self.slots + 1]
+
+    def permute(self, value, masks):
+        return lax.ppermute(value, AXES, [(i, i ^ masks[i & 1]) for i in range(self.devices)])
+
+    def swap(self, value):
+        return self.permute(value, (1, 1))
+
+    def lines(self):
+        return [[i + self.line * k for k in range(self.far)] for i in range(self.line)]
+
+    def gather_far(self, value):
+        masks = [(m * self.line, m * self.line) for m in range(1, self.far)]
+        return [value] + [self.permute(value, m) for m in masks]
+
+    def send_far(self, parts):
+        masks = [(m * self.line, m * self.line) for m in range(1, self.far)]
+        return [self.permute(v, m) for v, m in zip(parts[1:], masks)]
+
+
+def added(low, came):
+    return (low.astype(F32) + came.astype(F32)).astype(BF)
+
+
+def halves(low, came):
+    count = low.shape[0] // 2
+    return added(low[:count], came[:count]), added(low[count:], came[count:])
+
+
+def together(*lists):
+    flat = list(lax.optimization_barrier(tuple(v for values in lists for v in values)))
+    return [[flat.pop(0) for _ in values] for values in lists]
+
+
+def after_all(values, *others):
+    return lax.optimization_barrier(tuple(values) + others)[: len(values)]
+
+
+def after(value, *others):
+    return lax.optimization_barrier((value,) + others)[0] if others else value
+
+
+def mean(v):
+    return jnp.mean(v, -1, keepdims=True)
+
+
+def swap_lanes(v):
+    lane = lax.broadcasted_iota(jnp.int32, v.shape, 1)
+    return jnp.where(lane % 2 == 0, pltpu.roll(v, v.shape[1] - 1, 1), pltpu.roll(v, 1, 1))
+
+
+def first_half(rows):
+    return lax.broadcasted_iota(jnp.int32, (rows, 2 * HD), 1) < HD
+
+
+def fetch_attention(plan, table, h, pieces, triple, mix, sems, rows):
+    core = plan.core(table)
+    half_slots = plan.slots // 2
+    third = rows // 3
+    columns = pieces[2].shape[2]
+    for r in range(plan.slots):
+        chip = (plan.own, plan.other)[h](table, r)
+        side, at = divmod(r, half_slots)
+        first, second = pieces[side].at[at], pieces[2 + side].at[at]
+        if triple is not None:
+            pltpu.make_async_copy(
+                first.at[:, pl.ds(0, columns)],
+                triple.at[pl.ds(pl.multiple_of(chip * rows, 16), 2 * third)],
+                sems.at[0],
+            ).start()
+            pltpu.make_async_copy(
+                second.at[pl.ds(0, third)],
+                triple.at[pl.ds(pl.multiple_of(chip * rows + 2 * third, 16), third)],
+                sems.at[0],
+            ).start()
+        if mix is not None:
+            for b in range(3):
+                pltpu.make_async_copy(
+                    second.at[pl.ds(third, third), pl.ds(b * columns // 3, columns // 3)],
+                    mix.at[core ^ h, pl.ds(pl.multiple_of(chip * rows + b * third, 16), third)],
+                    sems.at[h],
+                ).start()
+
+
+def fetch_hidden(plan, table, pieces, weight, sems, rows, columns):
+    half_slots = plan.slots // 2
+    across = plan.narrow // 2
+    for h in (0, 1):
+        for r in range(plan.slots):
+            chip = (plan.own, plan.other)[h](table, r)
+            down, over = chip // across, chip % across
+            pltpu.make_async_copy(
+                pieces[2 * h + r // half_slots].at[r % half_slots],
+                weight.at[
+                    h,
+                    pl.ds(pl.multiple_of(down * rows, 16), rows),
+                    pl.ds(pl.multiple_of(over * columns, 128), columns),
+                ],
+                sems.at[h],
+            ).start()
+
+
+TRIPLE, MIX, GAIN1, SHIFT1, GAIN2, SHIFT2, UP = 0, 3, 4, 5, 6, 7, 8
+TABLE_ROWS = 16
+SHARE = 128
+
+
+def split_kernel(plan, index_ref, triple_ref, mix_ref, tb_ref, mb_ref, g1_ref, s1_ref, g2_ref,
+                 s2_ref, ub_ref, db_ref, mine_ref, share_ref, theirs_ref, spread):
+    index = index_ref[0]
+    core = index % 2
+    of_wide, of_narrow = index // plan.narrow, index % plan.narrow
+    triple, mix = triple_ref(), mix_ref()
+    width = mix.shape[1]
+    half = width // 2
+    for out, h in ((mine_ref, core), (theirs_ref, core ^ 1)):
+        for g in range(3):
+            at = pl.multiple_of(g * width + h * half, 128)
+            out[:, g * half : (g + 1) * half] = triple[:, pl.ds(at, half)]
+        out[:, 3 * half : 4 * half] = mix[:, pl.ds(pl.multiple_of(h * half, 128), half)]
+
+    spread[...] = jnp.zeros_like(spread)
+    for row, ref in ((TRIPLE, tb_ref), (MIX, mb_ref), (GAIN1, g1_ref), (SHIFT1, s1_ref),
+                     (GAIN2, g2_ref), (SHIFT2, s2_ref)):
+        spread[row : row + 1, : ref.shape[1]] = ref()[...].astype(F32)
+    for row, ref, which, parts in (
+        (UP, ub_ref, of_wide, plan.wide),
+        (UP + plan.narrow, db_ref, of_narrow, plan.narrow),
+    ):
+        count = ref.shape[1] // parts
+        values = ref()[...].astype(F32)
+        mine = jnp.zeros((1, count), F32)
+        for k in range(parts):
+            mine = jnp.where(which == k, values[:, k * count : (k + 1) * count], mine)
+        spread[row : row + 1, :count] = mine
+    share = spread[...].astype(BF)
+    share_ref[...] = share
+    theirs_ref[:TABLE_ROWS, 4 * half :] = share
+
+
+def join_kernel(plan, table, mine_ref, share_ref, came_ref, first_ref, second_ref):
+    core = plan.core(table)
+    half = mine_ref.shape[1] // 4
+    mine, came = mine_ref[...].astype(F32), came_ref[:, : 4 * half].astype(F32)
+    both = jnp.concatenate(
+        [jnp.where(core == 0, mine, came), jnp.where(core == 0, came, mine)], 0
+    ).astype(BF)
+    third = both.shape[0] // 3
+    first_ref[0, :, : 3 * half] = both[: 2 * third, : 3 * half]
+    second_ref[0, :third, :] = both[2 * third :, : 3 * half]
+    for b in range(3):
+        second_ref[0, third:, b * half : (b + 1) * half] = (
+            both[b * third : (b + 1) * third, 3 * half :]
+        )
+    share, other = share_ref[...], came_ref[:TABLE_ROWS, 4 * half :]
+    first_ref[0, :TABLE_ROWS, 3 * half :] = jnp.where(core == 0, share, other)
+    first_ref[0, TABLE_ROWS:, 3 * half :] = jnp.where(core == 0, other, share)
+
+
+def vectors_kernel(plan, share, table, low_ref, high_ref, out_ref, held, triple, plain, up, down,
+                   sem):
+    half_slots = plan.slots // 2
+    columns = low_ref.shape[2] - SHARE
+    for r in range(plan.slots):
+        pltpu.make_async_copy(
+            (low_ref, high_ref)[r // half_slots].at[r % half_slots, :, pl.ds(columns, SHARE)],
+            held.at[plan.own(table, r)],
+            sem.at[0],
+        ).start()
+    for ref in (triple, plain, up, down):
+        ref[...] = jnp.zeros_like(ref)
+    drain(held, sem.at[0])
+    width = out_ref.shape[1]
+    part = width // plan.wide
+
+    def put(ref, rows, at):
+        block, lane = divmod(at, SHARE)
+        s = slice(block * SHARE, (block + 2) * SHARE)
+        ref[..., s] = ref[..., s] + (pltpu.roll(rows, lane, 1) if lane else rows)
+
+    for device in range(plan.devices):
+        of_wide, of_narrow = divmod(device, plan.narrow)
+        rows = held[device // 2].astype(F32)[device % 2 * TABLE_ROWS :][:TABLE_ROWS]
+        rows = jnp.concatenate([rows, jnp.zeros_like(rows)], 1)
+        put(triple, rows[:8], 3 * share * device)
+        put(plain, rows[:8], share * device)
+        put(up.at[of_narrow], rows[8:], part * of_wide)
+        put(down, rows[8:], share * device)
+    out_ref[...] = jnp.zeros_like(out_ref)
+    for g in range(3):
+        out_ref[TRIPLE + g : TRIPLE + g + 1, :] = triple[0:1, g * width : (g + 1) * width]
+    out_ref[MIX:UP, :] = plain[MIX:UP, :width]
+    for n in range(plan.narrow):
+        out_ref[UP + n : UP + n + 1, :] = up[n, 0:1, :width]
+    row = UP + plan.narrow
+    out_ref[row : row + 1, :] = down[row - 8 : row - 7, :width]
+
+
+def pack_vectors(plan, core, width, bias_own, bias_other, first_ref, second_ref, up_ref, out_ref):
+    out_ref[...] = jnp.zeros_like(out_ref)
+    half = width // 2
+    for h, ref in ((0, bias_own), (1, bias_other)):
+        at = pl.ds(pl.multiple_of((core ^ h) * half, 128), half)
+        for g in range(3):
+            out_ref[TRIPLE + g : TRIPLE + g + 1, at] = ref[:, g * half : (g + 1) * half]
+    out_ref[MIX : MIX + 1, :width] = first_ref[2:3, :]
+    out_ref[GAIN1 : GAIN1 + 2, :width] = first_ref[0:2, :]
+    out_ref[GAIN2 : GAIN2 + 2, :width] = second_ref[0:2, :]
+    for h in (0, 1):
+        for y in range(plan.narrow // 2):
+            row = up_ref[h : h + 1, y * width : (y + 1) * width]
+            out_ref[pl.ds(UP + 2 * y + (core ^ h), 1), :width] = row
+    out_ref[UP + plan.narrow : UP + plan.narrow + 1, :width] = second_ref[2:3, :]
+
+
+def attention_kernel(plan, rows, h, table, x_ref, a, b, c, d, cos_ref, sin_ref, vec_ref,
+                     keep_ref, probs_ref, context_ref, triple, sems):
+    core, live = plan.core(table), plan.live(table)
+    tokens, width = x_ref.shape
+    half = width // 2
+    fetch_attention(plan, table, h, (a, b, c, d), triple, None, sems, rows)
+    x = x_ref()[...]
+    cos, sin = cos_ref[...], sin_ref[...]
+    left = first_half(tokens)
+    valid = lax.broadcasted_iota(jnp.int32, (1, tokens), 1) < live
+    scale = jnp.asarray(1.0 / math.sqrt(HD), BF)
+    drain(triple, sems.at[0])
+    for q in range(half // 128):
+        at = [slice(g * half + 128 * q, g * half + 128 * q + 128) for g in range(3)]
+        here = pl.ds(pl.multiple_of((core ^ h) * half + 128 * q, 128), 128)
+        out = [
+            nn(x, triple[:, s]) + vec_ref[TRIPLE + g : TRIPLE + g + 1, here]
+            for g, s in enumerate(at)
+        ]
+        query, key = [(v * cos + swap_lanes(v) * sin).astype(BF) for v in out[:2]]
+        value = out[2].astype(BF)
+        for s, v in zip(at, (query, key, value)):
+            keep_ref[:, s] = v
+        context = []
+        for e in (0, 1):
+            mine = left if e == 0 else ~left
+            masked = jnp.where(mine, query, jnp.zeros_like(query)) * scale
+            score = jnp.where(valid, nt(masked, key), -1e30)
+            power = jnp.exp(score - jnp.max(score, -1, keepdims=True))
+            prob = power * (1.0 / jnp.sum(power, -1, keepdims=True))
+            prob = prob.astype(BF)
+            probs_ref[2 * q + e] = prob
+            context.append(nn(prob, value))
+        context_ref[:, 128 * q : 128 * q + 128] = (
+            jnp.where(left, context[0], context[1]).astype(BF)
+        )
+
+
+def mix_kernel(plan, rows, table, x_ref, context_own, context_other, a, b, c, d, e, f, g, k,
+               vec_ref, unit_ref, inv_ref, low_ref, mix, sems):
+    core = plan.core(table)
+    half = context_own.shape[1]
+    for h, pieces in ((0, (a, b, c, d)), (1, (e, f, g, k))):
+        fetch_attention(plan, table, h, pieces, None, mix, sems, rows)
+    for h in (0, 1):
+        drain(mix.at[core ^ h], sems.at[h])
+    sides = []
+    for side in (0, 1):
+        total = 0.0
+        for h, context in ((0, context_own), (1, context_other)):
+            at = pl.ds(pl.multiple_of((core ^ h) * half, 128), half)
+            total = total + nn(context[...], mix[side, at, :])
+        sides.append(total)
+    branch = jnp.concatenate(sides, 1)
+    summed = x_ref()[...].astype(F32) + (branch + vec_ref[MIX : MIX + 1, :])
+    centred = summed - mean(summed)
+    inverse = lax.rsqrt(mean(centred * centred) + EPSILON)
+    unit = centred * inverse
+    unit_ref[...] = unit
+    inv_ref[...] = jnp.broadcast_to(inverse, inv_ref.shape)
+    low_ref[...] = (
+        unit * vec_ref[GAIN1 : GAIN1 + 1, :] + vec_ref[SHIFT1 : SHIFT1 + 1, :]
+    ).astype(BF)
+
+
+def up_kernel(plan, rows, columns, table, low_ref, a, b, c, d, vec_ref,
+              own_ref, other_ref, slope_own_ref, slope_other_ref, weight, sems):
+    fetch_hidden(plan, table, (a, b, c, d), weight, sems, rows, columns)
+    core = plan.core(table)
+    low = low_ref[...]
+    step = 256
+    for h, (out, slope) in enumerate(((own_ref, slope_own_ref), (other_ref, slope_other_ref))):
+        drain(weight.at[h], sems.at[h])
+        for k in range(out.shape[1] // step):
+            s = slice(k * step, (k + 1) * step)
+            y, at = divmod(k * step, columns)
+            row = vec_ref[pl.ds(UP + 2 * y + (core ^ h), 1), at : at + step]
+            up = nn(low, weight[h, :, s]) + row
+            share = 0.5 * (1.0 + lax.erf(up * math.sqrt(0.5)))
+            out[:, s] = (up * share).astype(BF)
+            slope[:, s] = (
+                share + up * jnp.exp(-0.5 * up * up) * (1.0 / math.sqrt(2.0 * math.pi))
+            ).astype(BF)
+
+
+def down_kernel(plan, rows, columns, table, act_own, act_other, a, b, c, d, unit_ref,
+                cot_ref, vec_ref, out_ref, grad_ref, grad_low_ref, sums_ref, weight, sems):
+    fetch_hidden(plan, table, (a, b, c, d), weight, sems, rows, columns)
+    first = (
+        unit_ref()[...] * vec_ref[GAIN1 : GAIN1 + 1, :] + vec_ref[SHIFT1 : SHIFT1 + 1, :]
+    )
+    cot = cot_ref()[...].astype(F32)
+    scaled = cot * vec_ref[GAIN2 : GAIN2 + 1, :]
+    scaled_mean = mean(scaled)
+    sums_ref[1:2, :] = jnp.sum(cot, 0, keepdims=True)
+    drain(weight.at[0], sems.at[0])
+    total = nt(act_own[...], weight[0])
+    drain(weight.at[1], sems.at[1])
+    total = total + nt(act_other[...], weight[1])
+    bias = vec_ref[UP + plan.narrow : UP + plan.narrow + 1, :]
+    summed = first + (total + bias)
+    centred = summed - mean(summed)
+    inverse = lax.rsqrt(mean(centred * centred) + EPSILON)
+    unit = centred * inverse
+    grad = inverse * (scaled - scaled_mean - unit * mean(scaled * unit))
+    grad_ref[...] = grad
+    low = grad.astype(BF)
+    grad_low_ref[...] = low
+    sums_ref[0:1, :] = jnp.sum(cot * unit, 0, keepdims=True)
+    sums_ref[2:3, :] = jnp.sum(low.astype(F32), 0, keepdims=True)
+    out_ref[...] = (
+        unit * vec_ref[GAIN2 : GAIN2 + 1, :] + vec_ref[SHIFT2 : SHIFT2 + 1, :]
+    ).astype(BF)
+
+
+def grad_up_kernel(plan, rows, columns, table, low_ref, a, b, c, d, slope_own, slope_other,
+                   own_ref, other_ref, sums_ref, weight, sems):
+    fetch_hidden(plan, table, (a, b, c, d), weight, sems, rows, columns)
+    low = low_ref[...]
+    step = 256
+    for h, slope, out in ((1, slope_other, other_ref), (0, slope_own, own_ref)):
+        drain(weight.at[h], sems.at[h])
+        slope = slope
+        for k in range(out.shape[1] // step):
+            s = slice(k * step, (k + 1) * step)
+            grad = (nn(low, weight[h, :, s]) * slope[:, s].astype(F32)).astype(BF)
+            out[:, s] = grad
+            sums_ref[h : h + 1, s] = jnp.sum(grad.astype(F32), 0, keepdims=True)
+
+
+def hidden_grad_kernel(plan, rows, columns, table, left_own, left_other, right_own,
+                       right_other, low_ref, high_ref, block, sems):
+    across, half_slots = plan.narrow // 2, plan.slots // 2
+    a, b = left_own[...], left_other[...]
+    for y in range(across):
+        s = slice(y * columns, (y + 1) * columns)
+        tile = tn(a, right_own[:, s]) + tn(b, right_other[:, s])
+        block[:, y] = tile.astype(BF).reshape(plan.wide, rows, columns)
+    for r in reversed(range(plan.slots)):
+        chip = plan.own(table, r)
+        out = (low_ref, high_ref)[r // half_slots]
+        pltpu.make_async_copy(
+            block.at[chip // across, chip % across], out.at[r % half_slots], sems.at[r // half_slots]
+        ).start()
+    drain(high_ref, sems.at[1])
+    drain(low_ref, sems.at[0])
+
+
+def first_grad_kernel(plan, rows, columns, arows, table, gu_own, gu_other, a, b, c, d,
+                      e, f, g, k, l, m, n, o, grad_ref, unit_ref, inv_ref, vec_ref, middle_ref,
+                      mine_ref, theirs_ref, context_ref, sums_ref, weight, sems, mix, mix_sems,
+                      low_ref):
+    fetch_hidden(plan, table, (a, b, c, d), weight, sems, rows, columns)
+    width = unit_ref.shape[1]
+    half = width // 2
+    for h, pieces in ((0, (e, f, g, k)), (1, (l, m, n, o))):
+        fetch_attention(plan, table, h, pieces, None, mix, mix_sems, arows)
+    core = plan.core(table)
+    drain(weight.at[0], sems.at[0])
+    total = nt(gu_own[...], weight[0])
+    drain(weight.at[1], sems.at[1])
+    total = total + nt(gu_other[...], weight[1])
+    grad = grad_ref()[...] + total
+    unit = unit_ref()[...]
+    scaled = grad * vec_ref[GAIN1 : GAIN1 + 1, :]
+    middle = inv_ref()[:, 0:1] * (scaled - mean(scaled) - unit * mean(scaled * unit))
+    low = middle.astype(BF)
+    middle_ref[...] = middle
+    low_ref[...] = low
+    mine_ref[...] = low_ref[:, pl.ds(pl.multiple_of(core * half, 128), half)]
+    theirs_ref[...] = low_ref[:, pl.ds(pl.multiple_of((core ^ 1) * half, 128), half)]
+    sums_ref[0:1, :] = jnp.sum(grad * unit, 0, keepdims=True)
+    sums_ref[1:2, :] = jnp.sum(grad, 0, keepdims=True)
+    sums_ref[2:3, :] = jnp.sum(low.astype(F32), 0, keepdims=True)
+    for h in (0, 1):
+        drain(mix.at[core ^ h], mix_sems.at[h])
+    context_ref[...] = (nt(low[:, :half], mix[0]) + nt(low[:, half:], mix[1])).astype(BF)
+
+
+def attention_grad_kernel(plan, h, table, keep_ref, probs_ref, grad_ref, cos_ref, sin_ref,
+                          out_ref, sums_ref):
+    core = plan.core(table)
+    tokens, width = grad_ref.shape
+    half = width // 2
+    cos, sin = cos_ref[...], sin_ref[...]
+    left = first_half(tokens)
+    scale = 1.0 / math.sqrt(HD)
+    keep, grads_in, probs = keep_ref(), grad_ref, probs_ref()
+    for q in range(half // 128):
+        at = [slice(g * half + 128 * q, g * half + 128 * q + 128) for g in range(3)]
+        query, key, value = [keep[:, s] for s in at]
+        came = grads_in[:, pl.ds(pl.multiple_of((core ^ h) * half + 128 * q, 128), 128)]
+        parts = []
+        for e in (0, 1):
+            mine = left if e == 0 else ~left
+            low = probs[2 * q + e]
+            prob = low.astype(F32)
+            grad = nt(jnp.where(mine, came, jnp.zeros_like(came)), value)
+            score = prob * (grad - jnp.sum(prob * grad, -1, keepdims=True))
+            score = score.astype(BF)
+            parts.append((nn(score, key), tn(score, query), tn(low, came)))
+        grads = [jnp.where(left, u, v) for u, v in zip(*parts)]
+        grads = [(g * scale) * cos + swap_lanes((g * scale) * sin) for g in grads[:2]] + grads[2:]
+        for s, g in zip(at, grads):
+            g = g.astype(BF)
+            out_ref[:, s] = g
+            sums_ref[:, s] = jnp.sum(g.astype(F32), 0, keepdims=True)
+
+
+def attention_weight_kernel(plan, rows, table, x_own, x_other, g_own, g_other, c_own, c_other,
+                            c_came_own, c_came_other, b_own, b_other, bias_own, bias_other,
+                            first_ref, second_ref, up_ref, low_ref, high_ref, block, mixed, sums,
+                            low_sums, sems):
+    core = plan.core(table)
+    half_slots = plan.slots // 2
+    tokens, columns = g_own.shape
+    third = columns // 3
+    height = rows + rows // 3
+    pack_vectors(
+        plan, core, x_own.shape[1], bias_own, bias_other, first_ref, second_ref, up_ref, sums
+    )
+    low_sums[...] = sums[...].astype(BF)
+    for ref, sem in ((high_ref, sems.at[1]), (low_ref, sems.at[0])):
+        pltpu.make_async_copy(
+            low_sums, ref.at[pl.ds(half_slots * height, TABLE_ROWS)], sem
+        ).start()
+    block[...] = (
+        (tn(x_own[...], g_own[...]) + tn(x_other[...], g_other[...]))
+        .astype(BF)
+        .reshape(block.shape)
+    )
+    for h, mine, came in ((0, c_own, c_came_other), (1, c_other, c_came_own)):
+        mixed[pl.ds((core ^ h) * half_slots, half_slots)] = (
+            (tn(mine[...], b_own[...]) + tn(came[...], b_other[...]))
+            .astype(BF)
+            .reshape((half_slots,) + mixed.shape[1:])
+        )
+    for r in reversed(range(plan.slots)):
+        chip = plan.own(table, r)
+        out, at = (low_ref, high_ref)[r // half_slots], r % half_slots * height
+        sem = sems.at[r // half_slots]
+        pltpu.make_async_copy(block.at[chip], out.at[pl.ds(at, rows)], sem).start()
+        for b in range(3):
+            pltpu.make_async_copy(
+                mixed.at[chip, b],
+                out.at[pl.ds(at + rows, rows // 3), pl.ds(b * third, third)],
+                sem,
+            ).start()
+    drain(high_ref, sems.at[1])
+    drain(low_ref, sems.at[0])
+
+
+def input_grad_kernel(plan, rows, table, middle_ref, g_own, g_other, a, b, c, d, e, f, g, k,
+                      out_ref, triple, sems):
+    for h, pieces in ((0, (a, b, c, d)), (1, (e, f, g, k))):
+        fetch_attention(plan, table, h, pieces, triple.at[h], None, sems.at[h], rows)
+    drain(triple.at[0], sems.at[0, 0])
+    total = nt(g_own[...], triple[0])
+    drain(triple.at[1], sems.at[1, 0])
+    total = total + nt(g_other[...], triple[1])
+    out_ref[...] = (middle_ref[...] + total).astype(BF)
+
+
+def half_tables(tokens):
+    position = jnp.arange(tokens, dtype=F32)
+    column = jnp.arange(2 * HD, dtype=jnp.int32)
+    pair = (column % HD // 2).astype(F32)
+    angle = position[:, None] * jnp.exp(pair * (-2.0 / HD) * math.log(10000.0))[None, :]
+    parity = (column % 2).astype(F32) * 2.0 - 1.0
+    return jnp.cos(angle), jnp.sin(angle) * parity[None, :]
+
+
+def fast_body(
+    plan,
+    inputs,
+    lengths,
+    triple_weight,
+    triple_bias,
+    mix_weight,
+    mix_bias,
+    first_gain,
+    first_shift,
+    up_weight,
+    up_bias,
+    down_weight,
+    down_bias,
+    second_gain,
+    second_shift,
+    cotangent,
+):
+    tokens, width = inputs.shape
+    half = width // 2
+    wide, narrow = plan.wide, plan.narrow
+    index = lax.axis_index(AXES)
+    core = index & 1
+    of_wide, of_narrow = lax.axis_index("wide"), lax.axis_index("narrow")
+    table = plan.table(index, lengths)
+    hidden = up_weight.shape[1]
+    tile_rows = up_weight.shape[0]
+    piece = triple_weight.shape[0]
+    rows = 2 * piece
+    third = rows // 3
+    half_slots = plan.slots // 2
+    flops = 2.0 * tokens * width * width
+    hidden_half = hidden * narrow // 2
+
+    def by_core(pair):
+        mine = jnp.where(core == 0, pair[0], pair[1])
+        theirs = jnp.where(core == 0, pair[1], pair[0])
+        return mine, theirs
+
+    def in_order(mine, theirs, axis):
+        return jnp.where(
+            core == 0,
+            jnp.concatenate([mine, theirs], axis),
+            jnp.concatenate([theirs, mine], axis),
+        )
+
+    row = functools.partial(jnp.reshape, shape=(1, -1))
+    mine, share, theirs = call(
+        functools.partial(split_kernel, plan),
+        [
+            shape((piece, 4 * half)),
+            shape((TABLE_ROWS, SHARE)),
+            shape((piece, 4 * half + SHARE)),
+        ],
+        (
+            index.astype(jnp.int32)[None],
+            triple_weight,
+            mix_weight,
+            row(triple_bias),
+            row(mix_bias),
+            row(first_gain),
+            row(first_shift),
+            row(second_gain),
+            row(second_shift),
+            row(up_bias),
+            row(down_bias),
+        ),
+        "s" + 10 * "l",
+        [VMEM((TABLE_ROWS, SHARE), F32)],
+        0,
+        60,
+    )
+    first, second = call(
+        functools.partial(join_kernel, plan),
+        [shape((1, 2 * third, 3 * half + SHARE)), shape((1, 2 * third, 3 * half))],
+        (table, mine, share, plan.swap(theirs)),
+        "svvv",
+        [],
+        0,
+        16,
+    )
+    cat = functools.partial(jnp.concatenate, axis=0)
+    cos, sin = half_tables(tokens)
+    first = cat(plan.gather_far(first))
+    came = plan.permute(first, plan.first)
+    second = plan.gather_far(after(second, first))
+    came, *second = after_all((came, *second))
+    first, second = cat((first, came)), cat(second)
+    first = (first, plan.permute(first, plan.last))
+    came = plan.permute(second, plan.first)
+    up = plan.gather_far(after(up_weight[None], second))
+    first, (came, cos, sin), up = together(first, (came, cos, sin), up)
+    second, up = cat((second, came)), cat(up)
+    second = (second, plan.permute(second, plan.last))
+    came = plan.permute(up, plan.first)
+    down = plan.gather_far(after(down_weight.T[None], up))
+    att_own, (came, up), down = together((*first, *second), (came, up), down)
+    down, up = cat(down), cat((up, came))
+    down_came = plan.permute(down, plan.first)
+    ups = (up, plan.permute(up, plan.last))
+    att_other = [plan.swap(v) for v in att_own]
+    (vecs,) = call(
+        functools.partial(vectors_kernel, plan, piece),
+        [shape((TABLE_ROWS, width), F32)],
+        (table, *att_own[:2]),
+        "shh",
+        [
+            VMEM((plan.slots, 2 * third, SHARE), BF),
+            VMEM((8, 3 * width + 2 * SHARE), F32),
+            VMEM((8, width + 2 * SHARE), F32),
+            VMEM((narrow, 8, width + 2 * SHARE), F32),
+            VMEM((8, width + 2 * SHARE), F32),
+            pltpu.SemaphoreType.DMA((1,)),
+        ],
+        0,
+        32,
+    )
+
+    def attend(h, pieces, gate=()):
+        return call(
+            functools.partial(attention_kernel, plan, rows, h),
+            [
+                shape((tokens, 3 * half)),
+                shape((half // HD, tokens, tokens)),
+                shape((tokens, half)),
+            ],
+            (after(table, *gate), inputs, *pieces, cos, sin, vecs),
+            "slhhhhvvv",
+            [VMEM((width, 3 * half), BF), pltpu.SemaphoreType.DMA((1,))],
+            1,
+            24,
+        )
+
+    own, p_own, context_own = attend(0, att_own, (up,))
+    down = cat(after_all((down, down_came), context_own))
+    downs = (down, plan.permute(down, plan.last))
+    other, p_other, context_other = attend(1, att_other, (down,))
+    ups = after_all(ups, context_other)
+    ups = (*ups, plan.swap(ups[0]), plan.swap(ups[1]))
+    unit, inv, low = call(
+        functools.partial(mix_kernel, plan, rows),
+        [shape((tokens, width), F32), shape((tokens, 128), F32), shape((tokens, width))],
+        (table, inputs, context_own, context_other, *att_own, *att_other, vecs),
+        "slvvhhhhhhhhv",
+        [VMEM((2, width, half), BF), pltpu.SemaphoreType.DMA((2,))],
+        1,
+        24,
+    )
+    hidden_scratch = [
+        VMEM((2, width, hidden_half), BF),
+        pltpu.SemaphoreType.DMA((2,)),
+    ]
+    act_own, act_other, slope_own, slope_other = call(
+        functools.partial(up_kernel, plan, tile_rows, hidden),
+        [shape((tokens, hidden_half))] * 4,
+        (table, low, *ups, vecs),
+        "svhhhhv",
+        hidden_scratch,
+        1,
+        24,
+    )
+    downs = after_all(downs, act_own)
+    downs = (*downs, plan.swap(downs[0]), plan.swap(downs[1]))
+    inputs_came, low_came, act_came = plan.swap(inputs), plan.swap(low), plan.swap(act_other)
+    context_came = plan.swap(context_own), plan.swap(context_other)
+    outputs, grad_second, grad_down, sums_second = call(
+        functools.partial(down_kernel, plan, tile_rows, hidden),
+        [
+            shape((tokens, width)),
+            shape((tokens, width), F32),
+            shape((tokens, width)),
+            shape((3, width), F32),
+        ],
+        (table, act_own, act_other, *downs, unit, cotangent, vecs),
+        "svvhhhhllv",
+        hidden_scratch,
+        1,
+        24,
+    )
+    grad_down_came = plan.swap(grad_down)
+    gu_own, gu_other, sums_up = call(
+        functools.partial(grad_up_kernel, plan, tile_rows, hidden),
+        [shape((tokens, hidden_half))] * 2 + [shape((2, hidden_half), F32)],
+        (table, grad_down, *downs, slope_own, slope_other),
+        "svhhhhvv",
+        hidden_scratch,
+        1,
+        24,
+    )
+    gu_came = plan.swap(gu_other)
+
+    def hidden_grad(left, left_came, right, right_came, gate):
+        return call(
+            functools.partial(hidden_grad_kernel, plan, tile_rows, hidden),
+            [shape((half_slots, tile_rows, hidden))] * 2,
+            (after(table, *gate), left, left_came, right, right_came),
+            "svvvv",
+            [VMEM((wide, narrow // 2, tile_rows, hidden), BF), pltpu.SemaphoreType.DMA((2,))],
+            1,
+            24,
+            [LEFT] * 2,
+        )
+
+    down_low, down_high = hidden_grad(grad_down, grad_down_came, act_own, act_came, (sums_up,))
+    down_came = plan.permute(down_high, plan.last)
+    up_low, up_high = hidden_grad(low, low_came, gu_own, gu_came, (down_low,))
+    up_came = plan.permute(up_high, plan.last)
+    grad_middle, branch_mine, branch_theirs, grad_context, sums_first = call(
+        functools.partial(first_grad_kernel, plan, tile_rows, hidden, rows),
+        [
+            shape((tokens, width), F32),
+            shape((tokens, half)),
+            shape((tokens, half)),
+            shape((tokens, width)),
+            shape((3, width), F32),
+        ],
+        (
+            after(table, up_low),
+            gu_own,
+            gu_other,
+            *ups,
+            *att_own,
+            *att_other,
+            grad_second,
+            unit,
+            inv,
+            vecs,
+        ),
+        "svvhhhhhhhhhhhhlllv",
+        hidden_scratch
+        + [
+            VMEM((2, width, half), BF),
+            pltpu.SemaphoreType.DMA((2,)),
+            VMEM((tokens, width), BF),
+        ],
+        1,
+        24,
+    )
+    branch_came = plan.swap(branch_theirs)
+
+    def attention_grad(h, keep, probs, gate=()):
+        return call(
+            functools.partial(attention_grad_kernel, plan, h),
+            [shape((tokens, 3 * half)), shape((1, 3 * half), F32)],
+            (after(table, *gate), keep, probs, grad_context, cos, sin),
+            "sllvvv",
+            [],
+            1,
+            24,
+        )
+
+    gt_other, bias_other = attention_grad(1, other, p_other)
+    gt_came = plan.swap(gt_other)
+    down_stay, down_away = halves(*after_all((down_low, down_came), bias_other))
+    down_came = plan.permute(down_away, plan.first)
+    gt_own, bias_own = attention_grad(0, own, p_own, (down_away,))
+    up_stay, up_away = halves(*after_all((up_low, up_came), bias_own))
+    up_came = plan.permute(up_away, plan.first)
+    height = rows + third
+    packed_low, packed_high = call(
+        functools.partial(attention_weight_kernel, plan, rows),
+        [shape((half_slots * height + TABLE_ROWS, 3 * half))] * 2,
+        (
+            after(table, up_away),
+            inputs,
+            inputs_came,
+            gt_own,
+            gt_came,
+            context_own,
+            context_other,
+            *context_came,
+            branch_mine,
+            branch_came,
+            bias_own,
+            bias_other,
+            sums_first,
+            sums_second,
+            sums_up,
+        ),
+        "s" + 15 * "v",
+        [
+            VMEM((plan.slots, rows, 3 * half), BF),
+            VMEM((plan.slots, 3, third, half), BF),
+            VMEM((TABLE_ROWS, 3 * half), F32),
+            VMEM((TABLE_ROWS, 3 * half), BF),
+            pltpu.SemaphoreType.DMA((2,)),
+        ],
+        80 * flops,
+        24,
+        [LEFT] * 2,
+    )
+    packed_came = plan.permute(packed_high, plan.last)
+    down_stay, down_came, up_stay, up_came = after_all(
+        (down_stay, down_came, up_stay, up_came), packed_low
+    )
+    near = [
+        jnp.stack([added(down_stay[k], down_came[k]), added(up_stay[k], up_came[k])])
+        for k in range(plan.far)
+    ]
+    near_came = plan.send_far(near)
+    (input_grad,) = call(
+        functools.partial(input_grad_kernel, plan, rows),
+        [shape((tokens, width))],
+        (after(table, near[0]), grad_middle, gt_own, gt_other, *att_own, *att_other),
+        "svvvhhhhhhhh",
+        [VMEM((2, width, 3 * half), BF), pltpu.SemaphoreType.DMA((2, 1))],
+        80 * flops,
+        40,
+    )
+    packed_low, packed_came = after_all((packed_low, packed_came), input_grad)
+    cut, end = half_slots // 2 * height, half_slots * height
+    sums = added(packed_low[end:], packed_came[end:])
+    packed_stay = added(packed_low[:cut], packed_came[:cut])
+    packed_away = cat([added(packed_low[cut:end], packed_came[cut:end]), sums])
+    packed_came = plan.permute(packed_away, plan.first)
+    (packed_came,) = after_all((packed_came,), *near_came)
+    total = sum([v.astype(F32) for v in near_came], near[0].astype(F32))
+    down_total, up_total = total[0], total[1]
+    sums = added(sums, packed_came[cut:])
+    parts = [
+        cat(
+            [
+                added(packed_stay[k * height :][:height], packed_came[k * height :][:height]),
+                sums,
+            ]
+        )
+        for k in range(plan.far)
+    ]
+    attention_total = sum([v.astype(F32) for v in plan.send_far(parts)], parts[0].astype(F32))
+    sums = attention_total[height:, :width]
+    flat = (sums + plan.swap(sums)).reshape(-1)
+
+    def share_of(row, at, count):
+        return lax.dynamic_slice(flat, (row * width + at * count,), (count,))
+
+    mix_rows = attention_total[rows:height].reshape(rows // 3, 3, half).transpose(1, 0, 2)
+    chip_grads = jnp.concatenate([attention_total[:rows], mix_rows.reshape(rows, half)], 1)
+    mine, theirs = by_core((chip_grads[:piece], chip_grads[piece:]))
+    came = plan.swap(theirs)
+    pair = in_order(mine[None], came[None], 0)
+    triple_grad = pair[:, :, : 3 * half].reshape(2, piece, 3, half).transpose(1, 2, 0, 3)
+    mix_grad = pair[:, :, 3 * half :].transpose(1, 0, 2)
+    return (
+        outputs,
+        input_grad,
+        triple_grad.reshape(piece, 3 * width),
+        share_of(TRIPLE, index, 3 * piece),
+        mix_grad.reshape(piece, width),
+        share_of(MIX, index, piece),
+        share_of(GAIN1, index, piece),
+        share_of(SHIFT1, index, piece),
+        up_total,
+        share_of(UP, of_narrow, hidden),
+        down_total.T,
+        share_of(UP + narrow, of_wide, down_bias.shape[0]),
+        share_of(GAIN2, index, piece),
+        share_of(SHIFT2, index, piece),
+    )
+
+
+def fits(plan_shape, width, hidden):
+    wide, narrow = plan_shape
+    powers = all(n >= 4 and n & (n - 1) == 0 for n in (wide, narrow)) and narrow == 4
+    return (
+        powers
+        and width % (wide * 16) == 0
+        and width % (wide * narrow // 2 * 48) == 0
+        and hidden % (narrow * 128) == 0
+        and width % 768 == 0
+    )
+
+
 def solution(mesh):
     placed = (
         P(("wide", "narrow"), None),
@@ -295,8 +1272,16 @@
         P(("wide", "narrow")),
         P(("wide", "narrow"), None),
     )
+    wide, narrow = mesh.shape["wide"], mesh.shape["narrow"]
+
+    def layer(*arrays):
+        rows, hidden = arrays[8].shape
+        if fits((wide, narrow), rows * wide, hidden * narrow):
+            return fast_body(Plan(wide, narrow), *arrays)
+        return body(*arrays)
+
     return jax.shard_map(
-        body,
+        layer,
         mesh=mesh,
         in_specs=placed,
         out_specs=(

time: 735 us -> 249 us (0.34); the launches traced: 723 us -> 245 us
  waiting for transfers between devices: 329 us -> 103 us
  blocking collectives: 139 us -> 0 us
  matrix products: 87.9 us -> 0 us
  local copies, waits for them, and re-layouts: 93.7 us -> 9.14 us
  Pallas kernels: 0 us -> 78.4 us
  other arithmetic: 55.5 us -> 4.18 us
  starting transfers between devices: 1.33 us -> 48.4 us
  between operations: 17.3 us -> 2.37 us
    unnamed x13 -> x0, waiting for transfers between devices: 128 us -> none
    all_gather x6 -> x0, waiting for transfers between devices: 121 us -> none  [the longest x1 29.8 us: body(): lax.all_gather(up_weight, 'wide', axis=0, tiled=True)]
    unnamed x4 -> x0, blocking collectives: 121 us -> none
    ppermute x0 -> x52, waiting for transfers between devices: none -> 103 us  [permute(): lax.ppermute(value, AXES, [(i, i ^ masks[i & 1]) for i in range(self.devi...]
    dot_general x17 -> x0, matrix products: 83.3 us -> none  [the longest x1 15 us: body(): jnp.dot(gathered, up_rows, preferred_element_type=jnp.float32)]
    reduce_scatter x5 -> x0, waiting for transfers between devices: 79.7 us -> none  [the longest x1 49.3 us: body(): lax.psum_scatter(mix_weight_grad, ('wide', 'narrow'), scatter_dimension=0...]
    pallas_call x0 -> x16, Pallas kernels: none -> 78.4 us  [call(): pl.pallas_call(whole, out_shape=outs, in_specs=[specs[kind] for kind in k...]
    ppermute x0 -> x52, starting transfers between devices: none -> 48.4 us  [permute(): lax.ppermute(value, AXES, [(i, i ^ masks[i & 1]) for i in range(self.devi...]
  transfers between devices with their start and end apart: 12 -> 52, of which waited for: 9 -> 21; matrix products, arithmetic and copies ran while one was open for 29% -> 3% of each run, Pallas kernels for 0% -> 31%
where the time goes in v1:
time: 249 us; the launch traced here: 245 us
  waiting for transfers between devices  103 us (41%)
  Pallas kernels  78.4 us (31%)
  starting transfers between devices  48.4 us (19%)
  local copies, waits for them, and re-layouts  9.14 us (4%)
  other arithmetic  4.18 us (2%)
    ppermute x52, waiting for transfers between devices, permute(): lax.ppermute(value, AXES, [(i, i ^ masks[i & 1]) for i in range(self.devi...  103 us
    pallas_call x16, Pallas kernels, call(): pl.pallas_call(whole, out_shape=outs, in_specs=[specs[kind] for kind in k...  78.4 us
    ppermute x52, starting transfers between devices, permute(): lax.ppermute(value, AXES, [(i, i ^ masks[i & 1]) for i in range(self.devi...  48.4 us
  transfers between devices with their start and end apart: 52, of which 21 were waited for; matrix products, arithmetic and copies ran while one was open for 3% of the time, Pallas kernels for 31%

profile of v1, /device:TPU:0, one launch (start us, length us, event | category | flops | bytes accessed | tf_op | source)
XLA Modules:
  0.0 245.2 jit_solution(1024822427704954244)
XLA Ops:
  1.9 2.2 shard_map.263
  8.3 2.7 %collective-permute-start.1 = (bf16[1,32,1280]{2,1,0:T(8,128)(2,1)S(1)}, bf16[1,32,1280]{2,1,0:T(8,128)(2,1)S(1)}, u32[]{:S(2)}, u32[]{:S(2)}) collective-permute-start(bf16[1,32,1280]{2,1,0:T(8,128)(2,1)S(1)} %get-tuple-element.109), channel_id=1, source_target_pairs={{0,8},{1,9},{2,10},{3,11},{4,12},{5,13},{6,14},{7,15},{8,0},{9,1},... | collective-permute-start | bytes 245768 | tf_op jit(solution)/shard_map/ppermute | solution.py:401
  11.0 2.7 %collective-permute-start.2 = (bf16[1,32,1280]{2,1,0:T(8,128)(2,1)S(1)}, bf16[1,32,1280]{2,1,0:T(8,128)(2,1)S(1)}, u32[]{:S(2)}, u32[]{:S(2)}) collective-permute-start(bf16[1,32,1280]{2,1,0:T(8,128)(2,1)S(1)} %get-tuple-element.109), channel_id=1, source_target_pairs={{0,16},{1,17},{2,18},{3,19},{4,20},{5,21},{6,22},{7,23},{8,24},{9,... | collective-permute-start | bytes 245768 | tf_op jit(solution)/shard_map/ppermute | solution.py:401
  14.0 6.5 %collective-permute-done.2 = bf16[1,32,1280]{2,1,0:T(8,128)(2,1)S(1)} collective-permute-done((bf16[1,32,1280]{2,1,0:T(8,128)(2,1)S(1)}, bf16[1,32,1280]{2,1,0:T(8,128)(2,1)S(1)}, u32[]{:S(2)}, u32[]{:S(2)}) %collective-permute-start.2) | collective-permute-done | bytes 81952 | tf_op jit(solution)/shard_map/ppermute | solution.py:401
  27.1 4.8 %collective-permute-done.6 = bf16[1,32,1152]{2,1,0:T(8,128)(2,1)S(1)} collective-permute-done((bf16[1,32,1152]{2,1,0:T(8,128)(2,1)S(1)}, bf16[1,32,1152]{2,1,0:T(8,128)(2,1)S(1)}, u32[]{:S(2)}, u32[]{:S(2)}) %collective-permute-start.6) | collective-permute-done | bytes 73760 | tf_op jit(solution)/shard_map/ppermute | solution.py:401
  40.8 7.8 %collective-permute-done.11 = bf16[1,96,768]{2,1,0:T(8,128)(2,1)S(1)} collective-permute-done((bf16[1,96,768]{2,1,0:T(8,128)(2,1)S(1)}, bf16[1,96,768]{2,1,0:T(8,128)(2,1)S(1)}, u32[]{:S(2)}, u32[]{:S(2)}) %collective-permute-start.11) | collective-permute-done | bytes 147488 | tf_op jit(solution)/shard_map/ppermute | solution.py:401
  50.8 2.1 collective-permute-start.15
  57.4 7.9 %collective-permute-done.16 = bf16[1,96,768]{2,1,0:T(8,128)(2,1)S(1)} collective-permute-done((bf16[1,96,768]{2,1,0:T(8,128)(2,1)S(1)}, bf16[1,96,768]{2,1,0:T(8,128)(2,1)S(1)}, u32[]{:S(2)}, u32[]{:S(2)}) %collective-permute-start.16) | collective-permute-done | bytes 147488 | tf_op jit(solution)/shard_map/ppermute | solution.py:401
  68.1 13.6 %collective-permute-done.18 = bf16[4,96,768]{2,1,0:T(8,128)(2,1)S(1)} collective-permute-done((bf16[4,96,768]{2,1,0:T(8,128)(2,1)S(1)}, bf16[4,96,768]{2,1,0:T(8,128)(2,1)S(1)}, u32[]{:S(2)}, u32[]{:S(2)}) %collective-permute-start.18) | collective-permute-done | bytes 589856 | tf_op jit(solution)/shard_map/ppermute | solution.py:401
  82.5 7.2 %shard_map.266 = (bf16[384,1152]{1,0:T(8,128)(2,1)S(1)}, bf16[6,384,384]{2,1,0:T(8,128)(2,1)S(1)}, bf16[384,384]{1,0:T(8,128)(2,1)S(1)}) custom-call(s32[34]{0:T(128)S(1)} %pad_add_fusion.refs_0_, bf16[384,768]{1,0:T(8,128)(2,1)S(1)} %copy-done, bf16[8,32,1280]{2,1,0:T(8,128)(2,1)S(1)} %constant_dynamic-update-slice_fusion.4.refs_1_.refs_2_.refs_4_.refs_7_, ...), custom_call_target="tpu_custom_call" | custom-call | flops 1 | bytes 1 | tf_op jit(solution)/shard_map/pallas_call | solution.py:342
  89.9 6.8 %shard_map.267 = (bf16[384,1152]{1,0:T(8,128)(2,1)S(1)}, bf16[6,384,384]{2,1,0:T(8,128)(2,1)S(1)}, bf16[384,384]{1,0:T(8,128)(2,1)S(1)}) custom-call(s32[34]{0:T(128)S(1)} %pad_add_fusion.refs_0_, bf16[384,768]{1,0:T(8,128)(2,1)S(1)} %copy-done, bf16[8,32,1280]{2,1,0:T(8,128)(2,1)S(1)} %collective-permute-done.19.refs_2_.refs_8_.refs_11_, ...), custom_call_target="tpu_custom_call" | custom-call | flops 1 | bytes 1 | tf_op jit(solution)/shard_map/pallas_call | solution.py:342
  97.8 3.0 %shard_map.268 = (f32[384,768]{1,0:T(8,128)S(1)}, f32[384,128]{1,0:T(8,128)S(1)}, bf16[384,768]{1,0:T(8,128)(2,1)S(1)}) custom-call(s32[34]{0:T(128)S(1)} %pad_add_fusion.refs_0_, bf16[384,768]{1,0:T(8,128)(2,1)S(1)} %copy-done, bf16[384,384]{1,0:T(8,128)(2,1)S(1)} %get-tuple-element.135.refs_2_.refs_5_, ...), custom_call_target="tpu_custom_call" | custom-call | flops 1 | bytes 1 | tf_op jit(solution)/shard_map/pallas_call | solution.py:342
  101.4 5.1 %shard_map.269 = (bf16[384,1536]{1,0:T(8,128)(2,1)S(1)}, bf16[384,1536]{1,0:T(8,128)(2,1)S(1)}, bf16[384,1536]{1,0:T(8,128)(2,1)S(1)}, bf16[384,1536]{1,0:T(8,128)(2,1)S(1)}) custom-call(s32[34]{0:T(128)S(1)} %pad_add_fusion.refs_0_, bf16[384,768]{1,0:T(8,128)(2,1)S(1)} %get-tuple-element.144.refs_1_, ...), custom_call_target="tpu_custom_call" | custom-call | flops 1 | bytes 1 | tf_op jit(solution)/shard_map/pallas_call | solution.py:342
  106.5 7.0 %collective-permute-done.26.refs_4_.refs_3_ = bf16[8,96,768]{2,1,0:T(8,128)(2,1)S(1)} collective-permute-done((bf16[8,96,768]{2,1,0:T(8,128)(2,1)S(1)}, bf16[8,96,768]{2,1,0:T(8,128)(2,1)S(1)}, u32[]{:S(2)}, u32[]{:S(2)}) %collective-permute-start.26) | collective-permute-done | bytes 1179680 | tf_op jit(solution)/shard_map/ppermute | solution.py:401
  114.0 2.3 collective-permute-done.27.refs_5_.refs_4_
  118.1 5.9 %shard_map.270 = (bf16[384,768]{1,0:T(8,128)(2,1)}, f32[384,768]{1,0:T(8,128)S(1)}, bf16[384,768]{1,0:T(8,128)(2,1)S(1)}, f32[3,768]{1,0:T(4,128)S(1)}) custom-call(s32[34]{0:T(128)S(1)} %pad_add_fusion.refs_0_, bf16[384,1536]{1,0:T(8,128)(2,1)S(1)} %get-tuple-element.147.refs_1_.refs_3_, bf16[384,1536]{1,0:T(8,128)(2,1)S(1)} %get-tuple-element.148.refs_2_, ...), custom_call_target="tpu_custom_call" | custom-call | flops 1 | bytes 1 | tf_op jit(solution)/shard_map/pallas_call | solution.py:342
  124.0 3.9 %shard_map.271 = (bf16[384,1536]{1,0:T(8,128)(2,1)S(1)}, bf16[384,1536]{1,0:T(8,128)(2,1)S(1)}, f32[2,1536]{1,0:T(2,128)S(1)}) custom-call(s32[34]{0:T(128)S(1)} %pad_add_fusion.refs_0_, bf16[384,768]{1,0:T(8,128)(2,1)S(1)} %get-tuple-element.153.refs_1_, bf16[8,96,768]{2,1,0:T(8,128)(2,1)S(1)} %constant_dynamic-update-slice_fusion.28.refs_3_.refs_2_, ...), custom_call_target="tpu_custom_call" | custom-call | flops 1 | bytes 1 | tf_op jit(solution)/shard_map/pallas_call | solution.py:342
  128.6 3.0 %collective-permute-done.29.refs_2_ = bf16[384,768]{1,0:T(8,128)(2,1)S(1)} collective-permute-done((bf16[384,768]{1,0:T(8,128)(2,1)S(1)}, bf16[384,768]{1,0:T(8,128)(2,1)S(1)}, u32[]{:S(2)}, u32[]{:S(2)}) %collective-permute-start.29) | collective-permute-done | bytes 589856 | tf_op jit(solution)/shard_map/ppermute | solution.py:401
  131.6 6.6 %shard_map.272 = (bf16[8,96,768]{2,1,0:T(8,128)(2,1)S(1)}, bf16[8,96,768]{2,1,0:T(8,128)(2,1)S(1)}) custom-call(s32[34]{0:T(128)S(1)} %pad_add_fusion.refs_0_, bf16[384,768]{1,0:T(8,128)(2,1)S(1)} %get-tuple-element.153.refs_1_, bf16[384,768]{1,0:T(8,128)(2,1)S(1)} %collective-permute-done.29.refs_2_, ...), custom_call_target="tpu_custom_call" | custom-call | flops 1 | bytes 1 | tf_op jit(solution)/shard_map/pallas_call | solution.py:342
  138.8 6.4 %shard_map.273 = (bf16[8,96,768]{2,1,0:T(8,128)(2,1)S(1)}, bf16[8,96,768]{2,1,0:T(8,128)(2,1)S(1)}) custom-call(s32[34]{0:T(128)S(1)} %pad_add_fusion.refs_0_, bf16[384,768]{1,0:T(8,128)(2,1)S(1)} %get-tuple-element.144.refs_1_, bf16[384,768]{1,0:T(8,128)(2,1)S(1)} %collective-permute-done.32.refs_2_, ...), custom_call_target="tpu_custom_call" | custom-call | flops 1 | bytes 1 | tf_op jit(solution)/shard_map/pallas_call | solution.py:342
  146.8 8.6 %shard_map.274 = (f32[384,768]{1,0:T(8,128)S(1)}, bf16[384,384]{1,0:T(8,128)(2,1)S(1)}, bf16[384,384]{1,0:T(8,128)(2,1)S(1)}, bf16[384,768]{1,0:T(8,128)(2,1)S(1)}, f32[3,768]{1,0:T(4,128)S(1)}) custom-call(s32[34]{0:T(128)S(1)} %pad_add_fusion.refs_0_, bf16[384,1536]{1,0:T(8,128)(2,1)S(1)} %get-tuple-element.163.refs_3_.refs_1_, ...), custom_call_target="tpu_custom_call" | custom-call | flops 1 | bytes 1 | tf_op jit(solution)/shard_map/pallas_call | solution.py:342
  155.5 4.5 %shard_map.275 = (bf16[384,1152]{1,0:T(8,128)(2,1)S(1)}, f32[1,1152]{1,0:T(1,128)S(1)}) custom-call(s32[34]{0:T(128)S(1)} %pad_add_fusion.refs_0_, bf16[384,1152]{1,0:T(8,128)(2,1)S(1)} %get-tuple-element.160.refs_1_, bf16[6,384,384]{2,1,0:T(8,128)(2,1)S(1)} %get-tuple-element.161.refs_2_, bf16[384,768]{1,0:T(8,128)(2,1)S(1)} %get-tuple-element.169.refs_3_, ...), custom_call_target="tpu_custom_call" | custom-call | flops 1 | bytes 1 | tf_op jit(solution)/shard_map/pallas_call | solution.py:342
  161.1 6.0 %collective-permute-done.35 = bf16[8,96,768]{2,1,0:T(8,128)(2,1)S(1)} collective-permute-done((bf16[8,96,768]{2,1,0:T(8,128)(2,1)S(1)}, bf16[8,96,768]{2,1,0:T(8,128)(2,1)S(1)}, u32[]{:S(2)}, u32[]{:S(2)}) %collective-permute-start.35) | collective-permute-done | bytes 1179680 | tf_op jit(solution)/shard_map/ppermute | solution.py:401
  167.5 4.8 %shard_map.276 = (bf16[384,1152]{1,0:T(8,128)(2,1)S(1)}, f32[1,1152]{1,0:T(1,128)S(1)}) custom-call(s32[34]{0:T(128)S(1)} %pad_add_fusion.refs_0_, bf16[384,1152]{1,0:T(8,128)(2,1)S(1)} %get-tuple-element.175.refs_1_, bf16[6,384,384]{2,1,0:T(8,128)(2,1)S(1)} %get-tuple-element.176.refs_2_, bf16[384,768]{1,0:T(8,128)(2,1)S(1)} %get-tuple-element.169.refs_3_, ...), custom_call_target="tpu_custom_call" | custom-call | flops 1 | bytes 1 | tf_op jit(solution)/shard_map/pallas_call | solution.py:342
  174.7 6.2 %shard_map.277 = (bf16[528,1152]{1,0:T(8,128)(2,1)S(1)}, bf16[528,1152]{1,0:T(8,128)(2,1)S(1)}) custom-call(s32[34]{0:T(128)S(1)} %pad_add_fusion.refs_0_, bf16[384,768]{1,0:T(8,128)(2,1)S(1)} %copy-done, bf16[384,768]{1,0:T(8,128)(2,1)S(1)} %collective-permute-done.37.refs_2_, bf16[384,1152]{1,0:T(8,128)(2,1)S(1)} %get-tuple-element.181.refs_3_.refs_2_, ...), custom_call_target="tpu_custom_call" | custom-call | flops 36238786560 | bytes 1 | tf_op jit(solution)/shard_map/pallas_call | solution.py:342
  181.4 5.7 %shard_map.278 = bf16[384,768]{1,0:T(8,128)(2,1)} custom-call(s32[34]{0:T(128)S(1)} %pad_add_fusion.refs_0_, f32[384,768]{1,0:T(8,128)S(1)} %get-tuple-element.193.refs_1_, bf16[384,1152]{1,0:T(8,128)(2,1)S(1)} %get-tuple-element.181.refs_3_.refs_2_, bf16[384,1152]{1,0:T(8,128)(2,1)S(1)} %get-tuple-element.182.refs_3_, ...), custom_call_target="tpu_custom_call" | custom-call | flops 36238786560 | bytes 1 | tf_op jit(solution)/shard_map/pallas_call | solution.py:342
  187.2 7.0 %collective-permute-done.36 = bf16[4,96,768]{2,1,0:T(8,128)(2,1)S(1)} collective-permute-done((bf16[4,96,768]{2,1,0:T(8,128)(2,1)S(1)}, bf16[4,96,768]{2,1,0:T(8,128)(2,1)S(1)}, u32[]{:S(2)}, u32[]{:S(2)}) %collective-permute-start.36) | collective-permute-done | bytes 589856 | tf_op jit(solution)/shard_map/ppermute | solution.py:401
  198.9 2.5 %collective-permute-done.42 = bf16[528,1152]{1,0:T(8,128)(2,1)S(1)} collective-permute-done((bf16[528,1152]{1,0:T(8,128)(2,1)S(1)}, bf16[528,1152]{1,0:T(8,128)(2,1)S(1)}, u32[]{:S(2)}, u32[]{:S(2)}) %collective-permute-start.42) | collective-permute-done | bytes 1216544 | tf_op jit(solution)/shard_map/ppermute | solution.py:401
  206.4 15.7 %collective-permute-done.45 = bf16[2,96,768]{2,1,0:T(8,128)(2,1)S(1)} collective-permute-done((bf16[2,96,768]{2,1,0:T(8,128)(2,1)}, bf16[2,96,768]{2,1,0:T(8,128)(2,1)S(1)}, u32[]{:S(2)}, u32[]{:S(2)}) %collective-permute-start.45) | collective-permute-done | bytes 294944 | tf_op jit(solution)/shard_map/ppermute | solution.py:401
  222.6 2.7 %collective-permute-start.48 = (bf16[80,1152]{1,0:T(8,128)(2,1)S(1)}, bf16[80,1152]{1,0:T(8,128)(2,1)S(1)}, u32[]{:S(2)}, u32[]{:S(2)}) collective-permute-start(bf16[80,1152]{1,0:T(8,128)(2,1)S(1)} %get-tuple-element.242), channel_id=1, source_target_pairs={{0,16},{1,17},{2,18},{3,19},{4,20},{5,21},{6,22},{7,23},{8,24},{9,... | collective-permute-start | bytes 552968 | tf_op jit(solution)/shard_map/ppermute | solution.py:401
  227.9 4.3 %collective-permute-done.47 = bf16[80,1152]{1,0:T(8,128)(2,1)S(1)} collective-permute-done((bf16[80,1152]{1,0:T(8,128)(2,1)S(1)}, bf16[80,1152]{1,0:T(8,128)(2,1)S(1)}, u32[]{:S(2)}, u32[]{:S(2)}) %collective-permute-start.47) | collective-permute-done | bytes 184352 | tf_op jit(solution)/shard_map/ppermute | solution.py:401
  232.2 6.9 %collective-permute-done.48 = bf16[80,1152]{1,0:T(8,128)(2,1)S(1)} collective-permute-done((bf16[80,1152]{1,0:T(8,128)(2,1)S(1)}, bf16[80,1152]{1,0:T(8,128)(2,1)S(1)}, u32[]{:S(2)}, u32[]{:S(2)}) %collective-permute-start.48) | collective-permute-done | bytes 184352 | tf_op jit(solution)/shard_map/ppermute | solution.py:401
  (162 shorter events, 60.3 us)
Async XLA Ops:
  20.6 11.3 %collective-permute-start.4 = (bf16[4,32,1280]{2,1,0:T(8,128)(2,1)S(1)}, bf16[4,32,1280]{2,1,0:T(8,128)(2,1)S(1)}, u32[]{:S(2)}, u32[]{:S(2)}) collective-permute-start(bf16[4,32,1280]{2,1,0:T(8,128)(2,1)S(1)} %get-tuple-element.220), channel_id=1, source_target_pairs={{0,4},{1,3},{2,6},{3,1},{4,0},{5,7},{6,2},{7,5},{8,12},{9,11},{10,... | collective-permute-start | bytes 983048 | tf_op jit(solution)/shard_map/ppermute | solution.py:401
  31.9 16.6 %collective-permute-start.8 = (bf16[8,32,1280]{2,1,0:T(8,128)(2,1)S(1)}, bf16[8,32,1280]{2,1,0:T(8,128)(2,1)S(1)}, u32[]{:S(2)}, u32[]{:S(2)}) collective-permute-start(bf16[8,32,1280]{2,1,0:T(8,128)(2,1)S(1)} %constant_dynamic-update-slice_fusion.4.refs_1_.refs_2_.refs_4_.refs_7_), channel_id=1, source_target_pairs={{0,2},{1,5},{2,0},{3,7},{4,6},{5,1},{6,4},{7,3},{8,10},{9,13},{10,... | collective-permute-start | bytes 1966088 | tf_op jit(solution)/shard_map/ppermute | solution.py:401
  33.4 15.1 %collective-permute-start.9 = (bf16[4,32,1152]{2,1,0:T(8,128)(2,1)S(1)}, bf16[4,32,1152]{2,1,0:T(8,128)(2,1)S(1)}, u32[]{:S(2)}, u32[]{:S(2)}) collective-permute-start(bf16[4,32,1152]{2,1,0:T(8,128)(2,1)S(1)} %get-tuple-element.229), channel_id=1, source_target_pairs={{0,4},{1,3},{2,6},{3,1},{4,0},{5,7},{6,2},{7,5},{8,12},{9,11},{10,... | collective-permute-start | bytes 884744 | tf_op jit(solution)/shard_map/ppermute | solution.py:401
  35.6 12.9 %collective-permute-start.11 = (bf16[1,96,768]{2,1,0:T(8,128)(2,1)S(1)}, bf16[1,96,768]{2,1,0:T(8,128)(2,1)S(1)}, u32[]{:S(2)}, u32[]{:S(2)}) collective-permute-start(bf16[1,96,768]{2,1,0:T(8,128)(2,1)S(1)} %bitcast.35), channel_id=1, source_target_pairs={{0,16},{1,17},{2,18},{3,19},{4,20},{5,21},{6,22},{7,23},{8,24},{9,... | collective-permute-start | bytes 442376 | tf_op jit(solution)/shard_map/ppermute | solution.py:401
  36.9 11.7 %collective-permute-start.12 = (bf16[1,96,768]{2,1,0:T(8,128)(2,1)S(1)}, bf16[1,96,768]{2,1,0:T(8,128)(2,1)S(1)}, u32[]{:S(2)}, u32[]{:S(2)}) collective-permute-start(bf16[1,96,768]{2,1,0:T(8,128)(2,1)S(1)} %bitcast.36), channel_id=1, source_target_pairs={{0,24},{1,25},{2,26},{3,27},{4,28},{5,29},{6,30},{7,31},{8,16},{9,... | collective-permute-start | bytes 442376 | tf_op jit(solution)/shard_map/ppermute | solution.py:401
  48.6 16.7 %collective-permute-start.14 = (bf16[4,96,768]{2,1,0:T(8,128)(2,1)S(1)}, bf16[4,96,768]{2,1,0:T(8,128)(2,1)S(1)}, u32[]{:S(2)}, u32[]{:S(2)}) collective-permute-start(bf16[4,96,768]{2,1,0:T(8,128)(2,1)S(1)} %constant_dynamic-update-slice_fusion.18), channel_id=1, source_target_pairs={{0,4},{1,3},{2,6},{3,1},{4,0},{5,7},{6,2},{7,5},{8,12},{9,11},{10,... | collective-permute-start | bytes 1769480 | tf_op jit(solution)/shard_map/ppermute | solution.py:401
  48.8 16.5 %collective-permute-start.13 = (bf16[8,32,1152]{2,1,0:T(8,128)(2,1)S(1)}, bf16[8,32,1152]{2,1,0:T(8,128)(2,1)S(1)}, u32[]{:S(2)}, u32[]{:S(2)}) collective-permute-start(bf16[8,32,1152]{2,1,0:T(8,128)(2,1)S(1)} %constant_dynamic-update-slice_fusion.13.refs_4_.refs_6_.refs_9_), channel_id=1, source_target_pairs={{0,2},{1,5},{2,0},{3,7},{4,6},{5,1},{6,4},{7,3},{8,10},{9,13},{10,... | collective-permute-start | bytes 1769480 | tf_op jit(solution)/shard_map/ppermute | solution.py:401
  52.9 12.3 %collective-permute-start.16 = (bf16[1,96,768]{2,1,0:T(8,128)(2,1)S(1)}, bf16[1,96,768]{2,1,0:T(8,128)(2,1)S(1)}, u32[]{:S(2)}, u32[]{:S(2)}) collective-permute-start(bf16[1,96,768]{2,1,0:T(8,128)(2,1)S(1)} %bitcast.39), channel_id=1, source_target_pairs={{0,16},{1,17},{2,18},{3,19},{4,20},{5,21},{6,22},{7,23},{8,24},{9,... | collective-permute-start | bytes 442376 | tf_op jit(solution)/shard_map/ppermute | solution.py:401
  53.7 11.5 %collective-permute-start.17 = (bf16[1,96,768]{2,1,0:T(8,128)(2,1)S(1)}, bf16[1,96,768]{2,1,0:T(8,128)(2,1)S(1)}, u32[]{:S(2)}, u32[]{:S(2)}) collective-permute-start(bf16[1,96,768]{2,1,0:T(8,128)(2,1)S(1)} %bitcast.40), channel_id=1, source_target_pairs={{0,24},{1,25},{2,26},{3,27},{4,28},{5,29},{6,30},{7,31},{8,16},{9,... | collective-permute-start | bytes 442376 | tf_op jit(solution)/shard_map/ppermute | solution.py:401
  65.4 16.3 %collective-permute-start.18 = (bf16[4,96,768]{2,1,0:T(8,128)(2,1)S(1)}, bf16[4,96,768]{2,1,0:T(8,128)(2,1)S(1)}, u32[]{:S(2)}, u32[]{:S(2)}) collective-permute-start(bf16[4,96,768]{2,1,0:T(8,128)(2,1)S(1)} %constant_dynamic-update-slice_fusion.24), channel_id=1, source_target_pairs={{0,4},{1,3},{2,6},{3,1},{4,0},{5,7},{6,2},{7,5},{8,12},{9,11},{10,... | collective-permute-start | bytes 1769480 | tf_op jit(solution)/shard_map/ppermute | solution.py:401
  67.2 29.5 %collective-permute-start.23 = (bf16[8,96,768]{2,1,0:T(8,128)(2,1)S(1)}, bf16[8,96,768]{2,1,0:T(8,128)(2,1)S(1)}, u32[]{:S(2)}, u32[]{:S(2)}) collective-permute-start(bf16[8,96,768]{2,1,0:T(8,128)(2,1)S(1)} %constant_dynamic-update-slice_fusion.22.refs_2_.refs_3_), channel_id=1, source_target_pairs={{0,2},{1,5},{2,0},{3,7},{4,6},{5,1},{6,4},{7,3},{8,10},{9,13},{10,... | collective-permute-start | bytes 3538952 | tf_op jit(solution)/shard_map/ppermute | solution.py:401
  67.5 22.3 %collective-permute-start.19 = (bf16[8,32,1280]{2,1,0:T(8,128)(2,1)S(1)}, bf16[8,32,1280]{2,1,0:T(8,128)(2,1)S(1)}, u32[]{:S(2)}, u32[]{:S(2)}) collective-permute-start(bf16[8,32,1280]{2,1,0:T(8,128)(2,1)S(1)} %constant_dynamic-update-slice_fusion.4.refs_1_.refs_2_.refs_4_.refs_7_), channel_id=1, source_target_pairs={{0,1},{1,0},{2,3},{3,2},{4,5},{5,4},{6,7},{7,6},{8,9},{9,8},{10,11... | collective-permute-start | bytes 1966088 | tf_op jit(solution)/shard_map/ppermute | solution.py:401
  67.5 22.3 %collective-permute-start.20 = (bf16[8,32,1280]{2,1,0:T(8,128)(2,1)S(1)}, bf16[8,32,1280]{2,1,0:T(8,128)(2,1)S(1)}, u32[]{:S(2)}, u32[]{:S(2)}) collective-permute-start(bf16[8,32,1280]{2,1,0:T(8,128)(2,1)S(1)} %collective-permute-done.8.refs_2_.refs_3_.refs_5_.refs_8_), channel_id=1, source_target_pairs={{0,1},{1,0},{2,3},{3,2},{4,5},{5,4},{6,7},{7,6},{8,9},{9,8},{10,11... | collective-permute-start | bytes 1966088 | tf_op jit(solution)/shard_map/ppermute | solution.py:401
  68.1 21.8 %collective-permute-start.21 = (bf16[8,32,1152]{2,1,0:T(8,128)(2,1)S(1)}, bf16[8,32,1152]{2,1,0:T(8,128)(2,1)S(1)}, u32[]{:S(2)}, u32[]{:S(2)}) collective-permute-start(bf16[8,32,1152]{2,1,0:T(8,128)(2,1)S(1)} %constant_dynamic-update-slice_fusion.13.refs_4_.refs_6_.refs_9_), channel_id=1, source_target_pairs={{0,1},{1,0},{2,3},{3,2},{4,5},{5,4},{6,7},{7,6},{8,9},{9,8},{10,11... | collective-permute-start | bytes 1769480 | tf_op jit(solution)/shard_map/ppermute | solution.py:401
  97.3 16.2 %collective-permute-start.26 = (bf16[8,96,768]{2,1,0:T(8,128)(2,1)S(1)}, bf16[8,96,768]{2,1,0:T(8,128)(2,1)S(1)}, u32[]{:S(2)}, u32[]{:S(2)}) collective-permute-start(bf16[8,96,768]{2,1,0:T(8,128)(2,1)S(1)} %constant_dynamic-update-slice_fusion.28.refs_3_.refs_2_), channel_id=1, source_target_pairs={{0,2},{1,5},{2,0},{3,7},{4,6},{5,1},{6,4},{7,3},{8,10},{9,13},{10,... | collective-permute-start | bytes 3538952 | tf_op jit(solution)/shard_map/ppermute | solution.py:401
  114.0 14.5 %collective-permute-start.30 = (bf16[384,1536]{1,0:T(8,128)(2,1)S(1)}, bf16[384,1536]{1,0:T(8,128)(2,1)S(1)}, u32[]{:S(2)}, u32[]{:S(2)}) collective-permute-start(bf16[384,1536]{1,0:T(8,128)(2,1)S(1)} %get-tuple-element.148.refs_2_), channel_id=1, source_target_pairs={{0,1},{1,0},{2,3},{3,2},{4,5},{5,4},{6,7},{7,6},{8,9},{9,8},{10,11... | collective-permute-start | bytes 3538952 | tf_op jit(solution)/shard_map/ppermute | solution.py:401
  127.9 10.9 %collective-permute-start.33 = (bf16[384,1536]{1,0:T(8,128)(2,1)S(1)}, bf16[384,1536]{1,0:T(8,128)(2,1)S(1)}, u32[]{:S(2)}, u32[]{:S(2)}) collective-permute-start(bf16[384,1536]{1,0:T(8,128)(2,1)S(1)} %get-tuple-element.164.refs_2_), channel_id=1, source_target_pairs={{0,1},{1,0},{2,3},{3,2},{4,5},{5,4},{6,7},{7,6},{8,9},{9,8},{10,11... | collective-permute-start | bytes 3538952 | tf_op jit(solution)/shard_map/ppermute | solution.py:401
  138.2 22.4 %collective-permute-start.31 = (bf16[8,96,768]{2,1,0:T(8,128)(2,1)S(1)}, bf16[8,96,768]{2,1,0:T(8,128)(2,1)S(1)}, u32[]{:S(2)}, u32[]{:S(2)}) collective-permute-start(bf16[8,96,768]{2,1,0:T(8,128)(2,1)S(1)} %get-tuple-element.159), channel_id=1, source_target_pairs={{0,2},{1,5},{2,0},{3,7},{4,6},{5,1},{6,4},{7,3},{8,10},{9,13},{10,... | collective-permute-start | bytes 3538952 | tf_op jit(solution)/shard_map/ppermute | solution.py:401
  145.2 22.0 %collective-permute-start.35 = (bf16[8,96,768]{2,1,0:T(8,128)(2,1)S(1)}, bf16[8,96,768]{2,1,0:T(8,128)(2,1)S(1)}, u32[]{:S(2)}, u32[]{:S(2)}) collective-permute-start(bf16[8,96,768]{2,1,0:T(8,128)(2,1)S(1)} %get-tuple-element.173), channel_id=1, source_target_pairs={{0,2},{1,5},{2,0},{3,7},{4,6},{5,1},{6,4},{7,3},{8,10},{9,13},{10,... | collective-permute-start | bytes 3538952 | tf_op jit(solution)/shard_map/ppermute | solution.py:401
  160.0 14.7 %collective-permute-start.38 = (bf16[384,1152]{1,0:T(8,128)(2,1)S(1)}, bf16[384,1152]{1,0:T(8,128)(2,1)S(1)}, u32[]{:S(2)}, u32[]{:S(2)}) collective-permute-start(bf16[384,1152]{1,0:T(8,128)(2,1)S(1)} %get-tuple-element.182.refs_3_), channel_id=1, source_target_pairs={{0,1},{1,0},{2,3},{3,2},{4,5},{5,4},{6,7},{7,6},{8,9},{9,8},{10,11... | collective-permute-start | bytes 2654216 | tf_op jit(solution)/shard_map/ppermute | solution.py:401
  160.1 12.5 %collective-permute-start.37 = (bf16[384,768]{1,0:T(8,128)(2,1)S(1)}, bf16[384,768]{1,0:T(8,128)(2,1)S(1)}, u32[]{:S(2)}, u32[]{:S(2)}) collective-permute-start(bf16[384,768]{1,0:T(8,128)(2,1)S(1)} %copy-done), channel_id=1, source_target_pairs={{0,1},{1,0},{2,3},{3,2},{4,5},{5,4},{6,7},{7,6},{8,9},{9,8},{10,11... | collective-permute-start | bytes 1769480 | tf_op jit(solution)/shard_map/ppermute | solution.py:401
  160.6 13.7 %collective-permute-start.39 = (bf16[384,384]{1,0:T(8,128)(2,1)S(1)}, bf16[384,384]{1,0:T(8,128)(2,1)S(1)}, u32[]{:S(2)}, u32[]{:S(2)}) collective-permute-start(bf16[384,384]{1,0:T(8,128)(2,1)S(1)} %get-tuple-element.135.refs_2_.refs_5_), channel_id=1, source_target_pairs={{0,1},{1,0},{2,3},{3,2},{4,5},{5,4},{6,7},{7,6},{8,9},{9,8},{10,11... | collective-permute-start | bytes 884744 | tf_op jit(solution)/shard_map/ppermute | solution.py:401
  160.7 14.0 %collective-permute-start.40 = (bf16[384,384]{1,0:T(8,128)(2,1)S(1)}, bf16[384,384]{1,0:T(8,128)(2,1)S(1)}, u32[]{:S(2)}, u32[]{:S(2)}) collective-permute-start(bf16[384,384]{1,0:T(8,128)(2,1)S(1)} %get-tuple-element.143.refs_3_.refs_6_), channel_id=1, source_target_pairs={{0,1},{1,0},{2,3},{3,2},{4,5},{5,4},{6,7},{7,6},{8,9},{9,8},{10,11... | collective-permute-start | bytes 884744 | tf_op jit(solution)/shard_map/ppermute | solution.py:401
  172.6 14.6 %collective-permute-start.34 = (bf16[4,96,768]{2,1,0:T(8,128)(2,1)S(1)}, bf16[4,96,768]{2,1,0:T(8,128)(2,1)S(1)}, u32[]{:S(2)}, u32[]{:S(2)}) collective-permute-start(bf16[4,96,768]{2,1,0:T(8,128)(2,1)S(1)} %get-tuple-element.203), channel_id=1, source_target_pairs={{0,4},{1,3},{2,6},{3,1},{4,0},{5,7},{6,2},{7,5},{8,12},{9,11},{10,... | collective-permute-start | bytes 1769480 | tf_op jit(solution)/shard_map/ppermute | solution.py:401
  174.3 19.8 %collective-permute-start.36 = (bf16[4,96,768]{2,1,0:T(8,128)(2,1)S(1)}, bf16[4,96,768]{2,1,0:T(8,128)(2,1)S(1)}, u32[]{:S(2)}, u32[]{:S(2)}) collective-permute-start(bf16[4,96,768]{2,1,0:T(8,128)(2,1)S(1)} %get-tuple-element.201), channel_id=1, source_target_pairs={{0,4},{1,3},{2,6},{3,1},{4,0},{5,7},{6,2},{7,5},{8,12},{9,11},{10,... | collective-permute-start | bytes 1769480 | tf_op jit(solution)/shard_map/ppermute | solution.py:401
  180.9 20.5 %collective-permute-start.42 = (bf16[528,1152]{1,0:T(8,128)(2,1)S(1)}, bf16[528,1152]{1,0:T(8,128)(2,1)S(1)}, u32[]{:S(2)}, u32[]{:S(2)}) collective-permute-start(bf16[528,1152]{1,0:T(8,128)(2,1)S(1)} %get-tuple-element.194), channel_id=1, source_target_pairs={{0,2},{1,5},{2,0},{3,7},{4,6},{5,1},{6,4},{7,3},{8,10},{9,13},{10,... | collective-permute-start | bytes 3649544 | tf_op jit(solution)/shard_map/ppermute | solution.py:401
  194.5 11.9 %collective-permute-start.46 = (bf16[2,96,768]{2,1,0:T(8,128)(2,1)S(1)}, bf16[2,96,768]{2,1,0:T(8,128)(2,1)S(1)}, u32[]{:S(2)}, u32[]{:S(2)}) collective-permute-start(bf16[2,96,768]{2,1,0:T(8,128)(2,1)S(1)} %pad_maximum_fusion.8), channel_id=1, source_target_pairs={{0,24},{1,25},{2,26},{3,27},{4,28},{5,29},{6,30},{7,31},{8,16},{9,... | collective-permute-start | bytes 884744 | tf_op jit(solution)/shard_map/ppermute | solution.py:401
  197.2 24.9 %collective-permute-start.45 = (bf16[2,96,768]{2,1,0:T(8,128)(2,1)}, bf16[2,96,768]{2,1,0:T(8,128)(2,1)S(1)}, u32[]{:S(2)}, u32[]{:S(2)}) collective-permute-start(bf16[2,96,768]{2,1,0:T(8,128)(2,1)} %pad_maximum_fusion.7), channel_id=1, source_target_pairs={{0,16},{1,17},{2,18},{3,19},{4,20},{5,21},{6,22},{7,23},{8,24},{9,... | collective-permute-start | bytes 884744 | tf_op jit(solution)/shard_map/ppermute | solution.py:401
  201.8 20.5 %collective-permute-start.43 = (bf16[272,1152]{1,0:T(8,128)(2,1)S(1)}, bf16[272,1152]{1,0:T(8,128)(2,1)S(1)}, u32[]{:S(2)}, u32[]{:S(2)}) collective-permute-start(bf16[272,1152]{1,0:T(8,128)(2,1)S(1)} %pad_maximum_fusion), channel_id=1, source_target_pairs={{0,4},{1,3},{2,6},{3,1},{4,0},{5,7},{6,2},{7,5},{8,12},{9,11},{10,... | collective-permute-start | bytes 1880072 | tf_op jit(solution)/shard_map/ppermute | solution.py:401
  204.3 17.9 %collective-permute-start.44 = (bf16[2,96,768]{2,1,0:T(8,128)(2,1)}, bf16[2,96,768]{2,1,0:T(8,128)(2,1)S(1)}, u32[]{:S(2)}, u32[]{:S(2)}) collective-permute-start(bf16[2,96,768]{2,1,0:T(8,128)(2,1)} %pad_maximum_fusion.6), channel_id=1, source_target_pairs={{0,8},{1,9},{2,10},{3,11},{4,12},{5,13},{6,14},{7,15},{8,0},{9,1},... | collective-permute-start | bytes 884744 | tf_op jit(solution)/shard_map/ppermute | solution.py:401
  222.6 16.4 %collective-permute-start.48 = (bf16[80,1152]{1,0:T(8,128)(2,1)S(1)}, bf16[80,1152]{1,0:T(8,128)(2,1)S(1)}, u32[]{:S(2)}, u32[]{:S(2)}) collective-permute-start(bf16[80,1152]{1,0:T(8,128)(2,1)S(1)} %get-tuple-element.242), channel_id=1, source_target_pairs={{0,16},{1,17},{2,18},{3,19},{4,20},{5,21},{6,22},{7,23},{8,24},{9,... | collective-permute-start | bytes 552968 | tf_op jit(solution)/shard_map/ppermute | solution.py:401
  225.3 13.7 %collective-permute-start.49 = (bf16[80,1152]{1,0:T(8,128)(2,1)S(1)}, bf16[80,1152]{1,0:T(8,128)(2,1)S(1)}, u32[]{:S(2)}, u32[]{:S(2)}) collective-permute-start(bf16[80,1152]{1,0:T(8,128)(2,1)S(1)} %get-tuple-element.243), channel_id=1, source_target_pairs={{0,24},{1,25},{2,26},{3,27},{4,28},{5,29},{6,30},{7,31},{8,16},{9,... | collective-permute-start | bytes 552968 | tf_op jit(solution)/shard_map/ppermute | solution.py:401
  (26 other events, 190.9 us)
